TPU v7x, 256 devices: a whole 4x4x8 slice. The times are simulated.
256 devices in a mesh: dp: 16 (over x_lo, z), seq: 16 (over y, x_hi, core).
Axes of the slice: x: 4 (x_hi: 2, x_lo: 2; x = x_hi * 2 + x_lo), y: 4, z: 8, core: 2. Of those that a mesh axis runs over, the one named last changes fastest.
Arguments:
- queries: bfloat16 [32, 1024, 2048], P('dp', 'seq'), may hold values from -200 to 200
- keys: bfloat16 [32, 1024, 2048], P('dp', 'seq'), may hold values from -8 to 8, as said below
- values: bfloat16 [32, 1024, 2048], P('dp', 'seq'), may hold values from -100 to 100, as said below
- out_grad: bfloat16 [32, 1024, 2048], P('dp', 'seq'), may hold values from -6 to 6
- conv_weight: float32 [7, 2048], replicated, may hold values from -3 to 3
- conv_bias: float32 [2048], replicated, may hold values from -3 to 3
- gain: float32 [2048], replicated, may hold values from 0.1 to 1.9
Outputs:
- query_grad: bfloat16 [32, 1024, 2048], P('dp', 'seq')
- key_grad: bfloat16 [32, 1024, 2048], P('dp', 'seq')
- value_grad: bfloat16 [32, 1024, 2048], P('dp', 'seq')
- weight_grad: float32 [7, 2048], P(None, 'seq')
- bias_grad: float32 [2048], P('seq')
- gain_grad: float32 [2048], P('seq')
Inputs may be any that keep to these rules, and one draw needn't show every extreme that they name: keys of order one. values scaled by a factor for each frame and one for each channel.
All inputs are finite; a program needn't handle non-finite values.
Results may differ from a plain program's by a relative error of at most 0.024.
Values may be sent and summed in bfloat16 or wider, within the bound.
No kernel may reach another device: no remote copies, remote signals or barrier semaphores. Data moves between devices by JAX's collectives and lax.ppermute only.
A program may use at most 64 MiB of HBM per device.

v0:
```python
import math

import jax
import jax.numpy as jnp
from jax import lax
from jax.sharding import PartitionSpec as P

HDIM = 128


def padded_2(block, sides, width):
    for axis, dim in sides:
        count = lax.axis_size(axis)
        forward = [(i, i + 1) for i in range(count - 1)]
        backward = [(target, source) for source, target in forward]
        low = lax.ppermute(
            lax.slice_in_dim(block, block.shape[dim] - width, None, axis=dim), axis, forward
        )
        high = lax.ppermute(lax.slice_in_dim(block, 0, width, axis=dim), axis, backward)
        block = jnp.concatenate([low, block, high], axis=dim)
    return block


def split_heads(x):
    return x.reshape(x.shape[0], -1, HDIM)


def forward_heads(query_heads, key_heads, value_heads):
    scale = 1.0 / math.sqrt(HDIM)

    def forward_single(items):
        query, key, value = items
        scores = (
            jnp.einsum(
                "qhd,khd->hqk",
                split_heads(query),
                split_heads(key),
                preferred_element_type=jnp.float32,
            )
            * scale
        )
        top = jnp.max(scores, axis=-1, keepdims=True)
        lse = top + jnp.log(jnp.sum(jnp.exp(scores - top), axis=-1, keepdims=True))
        weights = jnp.exp(scores - lse).astype(jnp.bfloat16)
        out = jnp.einsum(
            "hqk,khd->qhd", weights, split_heads(value), preferred_element_type=jnp.float32
        )
        return (out.reshape(query.shape[0], -1).astype(jnp.bfloat16), lse)

    return lax.map(forward_single, (query_heads, key_heads, value_heads))


def backward_heads(query_heads, key_heads, value_heads, grad_heads, lse_all):
    scale = 1.0 / math.sqrt(HDIM)

    def backward_single(items):
        query, key, value, grad, lse = items
        q_split, k_split, v_split, g_split = (
            split_heads(query),
            split_heads(key),
            split_heads(value),
            split_heads(grad),
        )
        scores = (
            jnp.einsum("qhd,khd->hqk", q_split, k_split, preferred_element_type=jnp.float32) * scale
        )
        probs = jnp.exp(scores - lse)
        weights = probs.astype(jnp.bfloat16)
        value_grad = jnp.einsum(
            "hqk,qhd->khd", weights, g_split, preferred_element_type=jnp.float32
        )
        prob_grad = jnp.einsum("qhd,khd->hqk", g_split, v_split, preferred_element_type=jnp.float32)
        delta = jnp.sum(probs * prob_grad, axis=-1, keepdims=True)
        score_grad = (probs * (prob_grad - delta)).astype(jnp.bfloat16)
        query_grad = (
            jnp.einsum("hqk,khd->qhd", score_grad, k_split, preferred_element_type=jnp.float32)
            * scale
        )
        key_grad = (
            jnp.einsum("hqk,qhd->khd", score_grad, q_split, preferred_element_type=jnp.float32)
            * scale
        )
        rows = query.shape[0]
        return (
            query_grad.reshape(rows, -1).astype(jnp.bfloat16),
            key_grad.reshape(rows, -1).astype(jnp.bfloat16),
            value_grad.reshape(rows, -1).astype(jnp.bfloat16),
        )

    return lax.map(backward_single, (query_heads, key_heads, value_heads, grad_heads, lse_all))


def convolve(padded, taps_weight, bias_row, length):
    taps = taps_weight.shape[0]
    return bias_row[None, None, :] + sum(
        (taps_weight[t][None, None, :] * padded[:, t : t + length] for t in range(taps))
    )


def transpose_conv(grad_pad, taps_weight, length):
    taps = taps_weight.shape[0]
    half = taps // 2
    return sum(
        (
            taps_weight[t][None, None, :] * grad_pad[:, 2 * half - t : 2 * half - t + length]
            for t in range(taps)
        )
    )


def norm_grad(conv, upper, gain_row, sumsq, dot, width):
    ratio = lax.rsqrt(sumsq[..., None] / width + 1e-06)
    gain_term = jnp.sum(upper * conv * ratio, axis=(0, 1))
    conv_grad = ratio * gain_row[None, None, :] * upper - conv * ratio**3 * (dot[..., None] / width)
    return (conv_grad, gain_term)


def tap_terms(conv_grad, padded, taps, length):
    return jnp.stack(
        [jnp.sum(conv_grad * padded[:, t : t + length], axis=(0, 1)) for t in range(taps)]
    )


def per_device(queries, keys, values, out_grad, conv_weight, conv_bias, gain):
    width = queries.shape[2]
    taps = conv_weight.shape[0]
    half = taps // 2
    query_heads, key_heads, value_heads = (
        lax.all_to_all(queries, "seq", split_axis=2, concat_axis=1, tiled=True),
        lax.all_to_all(keys, "seq", split_axis=2, concat_axis=1, tiled=True),
        lax.all_to_all(values, "seq", split_axis=2, concat_axis=1, tiled=True),
    )
    attended, lse_all = forward_heads(query_heads, key_heads, value_heads)
    attended_frames = lax.all_to_all(attended, "seq", split_axis=1, concat_axis=2, tiled=True)
    length = attended_frames.shape[1]
    padded = padded_2(attended_frames, (("seq", 1),), half).astype(jnp.float32)
    conv = convolve(padded, conv_weight, conv_bias, length)
    upper = out_grad.astype(jnp.float32)
    sumsq = jnp.sum(conv * conv, axis=-1)
    dot = jnp.sum(conv * gain[None, None, :] * upper, axis=-1)
    conv_grad, gain_term = norm_grad(conv, upper, gain, sumsq, dot, width)
    grad_pad = padded_2(conv_grad, (("seq", 1),), half)
    back = transpose_conv(grad_pad, conv_weight, length)
    grad_frames = (upper + back).astype(jnp.bfloat16)
    grad_heads = lax.all_to_all(grad_frames, "seq", split_axis=2, concat_axis=1, tiled=True)
    weight_term = tap_terms(conv_grad, padded, taps, length)
    bias_term = jnp.sum(conv_grad, axis=(0, 1))
    weight_part, bias_part, gain_part = (
        lax.psum_scatter(
            weight_term.astype(jnp.bfloat16), "seq", scatter_dimension=1, tiled=True
        ).astype(jnp.float32),
        lax.psum_scatter(
            bias_term.astype(jnp.bfloat16), "seq", scatter_dimension=0, tiled=True
        ).astype(jnp.float32),
        lax.psum_scatter(
            gain_term.astype(jnp.bfloat16), "seq", scatter_dimension=0, tiled=True
        ).astype(jnp.float32),
    )
    weight_grad, bias_grad, gain_grad = lax.psum((weight_part, bias_part, gain_part), "dp")
    query_part, key_part, value_part = backward_heads(
        query_heads, key_heads, value_heads, grad_heads, lse_all
    )
    query_grad, key_grad, value_grad = (
        lax.all_to_all(query_part, "seq", split_axis=1, concat_axis=2, tiled=True),
        lax.all_to_all(key_part, "seq", split_axis=1, concat_axis=2, tiled=True),
        lax.all_to_all(value_part, "seq", split_axis=1, concat_axis=2, tiled=True),
    )
    return (query_grad, key_grad, value_grad, weight_grad, bias_grad, gain_grad)


def solution(mesh):
    in_specs = (
        P("dp", "seq", None),
        P("dp", "seq", None),
        P("dp", "seq", None),
        P("dp", "seq", None),
        P(),
        P(),
        P(),
    )
    out_specs = (
        P("dp", "seq", None),
        P("dp", "seq", None),
        P("dp", "seq", None),
        P(None, "seq"),
        P("seq"),
        P("seq"),
    )
    return jax.shard_map(
        per_device, mesh=mesh, in_specs=in_specs, out_specs=out_specs, check_vma=False
    )
```

profile of v0, /device:TPU:2, one launch (start us, length us, event | category | flops | bytes accessed | tf_op | source)
XLA Modules:
  0.0 306.7 jit_solution(9717919512730655031)
XLA Ops:
  7.2 2.4 copy.41
  11.1 6.1 %all-to-all-start = ((bf16[16,2,8192]{2,1,0:T(2,128)(2,1)}), bf16[16,2,8192]{2,1,0:T(2,128)(2,1)S(1)}, u32[]{:S(2)}, u32[]{:S(2)}) async-start(bf16[16,2,8192]{2,1,0:T(2,128)(2,1)} %reshape.222), calls=%async_computation | async-start | bytes 1048576 | tf_op jit(solution)/shard_map/all_to_all | solution.py:130
  19.6 10.1 %all-to-all-done = bf16[16,2,8192]{2,1,0:T(2,128)(2,1)S(1)} async-done(((bf16[16,2,8192]{2,1,0:T(2,128)(2,1)}), bf16[16,2,8192]{2,1,0:T(2,128)(2,1)S(1)}, u32[]{:S(2)}, u32[]{:S(2)}) %all-to-all-start) | async-done | bytes 524320 | tf_op jit(solution)/shard_map/all_to_all | solution.py:130
  29.7 3.6 %all-to-all-start.1 = ((bf16[16,2,8192]{2,1,0:T(2,128)(2,1)}), bf16[16,2,8192]{2,1,0:T(2,128)(2,1)S(1)}, u32[]{:S(2)}, u32[]{:S(2)}) async-start(bf16[16,2,8192]{2,1,0:T(2,128)(2,1)} %reshape.224), calls=%async_computation.1 | async-start | bytes 1048576 | tf_op jit(solution)/shard_map/all_to_all | solution.py:129
  35.5 10.0 %all-to-all-done.1 = bf16[16,2,8192]{2,1,0:T(2,128)(2,1)S(1)} async-done(((bf16[16,2,8192]{2,1,0:T(2,128)(2,1)}), bf16[16,2,8192]{2,1,0:T(2,128)(2,1)S(1)}, u32[]{:S(2)}, u32[]{:S(2)}) %all-to-all-start.1) | async-done | bytes 524320 | tf_op jit(solution)/shard_map/all_to_all | solution.py:129
  45.6 3.6 %all-to-all-start.2 = ((bf16[16,2,8192]{2,1,0:T(2,128)(2,1)}), bf16[16,2,8192]{2,1,0:T(2,128)(2,1)S(1)}, u32[]{:S(2)}, u32[]{:S(2)}) async-start(bf16[16,2,8192]{2,1,0:T(2,128)(2,1)} %reshape.226), calls=%async_computation.2 | async-start | bytes 1048576 | tf_op jit(solution)/shard_map/all_to_all | solution.py:131
  52.0 9.5 %all-to-all-done.2 = bf16[16,2,8192]{2,1,0:T(2,128)(2,1)S(1)} async-done(((bf16[16,2,8192]{2,1,0:T(2,128)(2,1)}), bf16[16,2,8192]{2,1,0:T(2,128)(2,1)S(1)}, u32[]{:S(2)}, u32[]{:S(2)}) %all-to-all-start.2) | async-done | bytes 524320 | tf_op jit(solution)/shard_map/all_to_all | solution.py:131
  63.0 4.9 %while.26 = (s32[]{:T(128)}, bf16[2,1024,128]{1,2,0:T(8,128)(2,1)S(1)}, f32[2,1,1024,1]{2,3,1,0:T(1,128)S(1)}, bf16[2,1024,128]{2,1,0:T(8,128)(2,1)S(1)}, bf16[2...) while((s32[]{:T(128)}, bf16[2,1024,128]{1,2,0:T(8,128)(2,1)S(1)}, ...), condition=%wide.region_3.4_spmd, body=%wide.region_0.3_spmd.sunk | while | flops 545389568 | bytes 13670481 | solution.py:50
  68.3 15.0 %all_to_all.144 = bf16[2,1024,128]{2,0,1:T(2,128)(2,1)S(1)} all-to-all(bf16[2,1024,128]{2,0,1:T(2,128)(2,1)S(1)} %copy.47), channel_id=1, replica_groups=mesh['dp'=16,'seq'=16] {'seq'}, dimensions={1} | all-to-all | bytes 1048576 | tf_op jit(solution)/shard_map/all_to_all | solution.py:134
  86.2 2.7 collective-permute-done.1
  93.3 6.9 %collective-permute-start.3 = (f32[2,3,2048]{2,1,0:T(4,128)S(1)}, f32[2,3,2048]{2,1,0:T(4,128)S(1)}, u32[]{:S(2)}, u32[]{:S(2)}) collective-permute-start(f32[2,3,2048]{2,1,0:T(4,128)S(1)} %get-tuple-element.146), channel_id=1, source_target_pairs={{0,1},{1,2},{2,3},{3,4},{4,5},{5,6},{6,7},{7,8},{8,9},{9,10},{10,1... | collective-permute-start | bytes 147464 | tf_op jit(solution)/shard_map/ppermute | solution.py:16
  103.3 23.7 %all_to_all.145 = bf16[16,2,8192]{2,1,0:T(2,128)(2,1)S(1)} all-to-all(bf16[16,2,8192]{2,1,0:T(2,128)(2,1)S(1)} %reshape.228), channel_id=1, replica_groups=mesh['dp'=16,'seq'=16] {'seq'}, dimensions={0} | all-to-all | bytes 1048576 | tf_op jit(solution)/shard_map/all_to_all | solution.py:145
  129.5 11.7 %while.27 = (s32[]{:T(128)}, bf16[2,1024,128]{1,2,0:T(8,128)(2,1)S(1)}, bf16[2,1024,128]{1,2,0:T(8,128)(2,1)S(1)}, bf16[2,1024,128]{1,2,0:T(8,128)(2,1)}, bf16[2...) while((s32[]{:T(128)}, ...), condition=%wide.region_8.9_spmd, body=%wide.region_6.8_spmd.sunk | while | flops 1355414528 | bytes 34112616 | solution.py:90
  133.7 1.6 fusion.112
  139.5 1.6 fusion.112
  141.2 2.0 copy.58
  143.2 3.6 %all-to-all-start.7 = ((bf16[2,1024,128]{2,0,1:T(2,128)(2,1)}), bf16[2,1024,128]{2,0,1:T(2,128)(2,1)S(1)}, u32[]{:S(2)}, u32[]{:S(2)}) async-start(bf16[2,1024,128]{2,0,1:T(2,128)(2,1)} %copy.58), calls=%async_computation.7 | async-start | bytes 1048576 | tf_op jit(solution)/shard_map/all_to_all | solution.py:166
  147.9 11.2 %all-to-all-done.7 = bf16[2,1024,128]{2,0,1:T(2,128)(2,1)S(1)} async-done(((bf16[2,1024,128]{2,0,1:T(2,128)(2,1)}), bf16[2,1024,128]{2,0,1:T(2,128)(2,1)S(1)}, u32[]{:S(2)}, u32[]{:S(2)}) %all-to-all-start.7) | async-done | bytes 524320 | tf_op jit(solution)/shard_map/all_to_all | solution.py:166
  159.1 3.6 %all-to-all-start.6 = ((bf16[2,1024,128]{2,0,1:T(2,128)(2,1)}), bf16[2,1024,128]{2,0,1:T(2,128)(2,1)S(1)}, u32[]{:S(2)}, u32[]{:S(2)}) async-start(bf16[2,1024,128]{2,0,1:T(2,128)(2,1)} %copy.55), calls=%async_computation.6 | async-start | bytes 1048576 | tf_op jit(solution)/shard_map/all_to_all | solution.py:165
  163.8 11.2 %all-to-all-done.6 = bf16[2,1024,128]{2,0,1:T(2,128)(2,1)S(1)} async-done(((bf16[2,1024,128]{2,0,1:T(2,128)(2,1)}), bf16[2,1024,128]{2,0,1:T(2,128)(2,1)S(1)}, u32[]{:S(2)}, u32[]{:S(2)}) %all-to-all-start.6) | async-done | bytes 524320 | tf_op jit(solution)/shard_map/all_to_all | solution.py:165
  175.0 3.6 %all-to-all-start.5 = ((bf16[2,1024,128]{2,0,1:T(2,128)(2,1)}), bf16[2,1024,128]{2,0,1:T(2,128)(2,1)S(1)}, u32[]{:S(2)}, u32[]{:S(2)}) async-start(bf16[2,1024,128]{2,0,1:T(2,128)(2,1)} %copy.52), calls=%async_computation.5 | async-start | bytes 1048576 | tf_op jit(solution)/shard_map/all_to_all | solution.py:164
  181.2 38.9 %all-reduce.3 = (bf16[2048]{0:T(1024)(128)(2,1)S(1)}, bf16[2048]{0:T(1024)(128)(2,1)S(1)}) all-reduce(bf16[2048]{0:T(1024)(128)(2,1)S(1)} %get-tuple-element.102, bf16[2048]{0:T(1024)(128)(2,1)S(1)} %get-tuple-element.100), channel_id=3, replica_groups=mesh['dp'=16,'seq'=16] {'seq'}, use_global_device_ids=true, to_apply=%region_19.20.clone | all-reduce | flops 4096 | bytes 16384
  220.2 40.2 %reduce-scatter.4.cloned.1.call-done = bf16[128,7]{1,0:T(8,128)(2,1)} async-done(((bf16[2048,7]{1,0:T(8,128)(2,1)}), bf16[128,7]{1,0:T(8,128)(2,1)}) %reduce-scatter.4.cloned.1.call-update) | async-done | bytes 1808
  261.2 35.7 %all-reduce.2 = (f32[7,128]{1,0:T(8,128)}, f32[128]{0:T(128)}, f32[128]{0:T(128)}) all-reduce(bf16[7,128]{1,0:T(8,128)(2,1)S(1)} %copy.62, f32[128]{0:T(128)S(1)} %get-tuple-element.159, f32[128]{0:T(128)S(1)} %get-tuple-element.158), channel_id=1, replica_groups=mesh['dp'=16,'seq'=16] {'dp'}, use_global_device_ids=true, to_apply=%region_17.18 | all-reduce | flops 1152 | bytes 7424 | tf_op jit(solution)/shard_map/psum | solution.py:159
  (98 shorter events, 44.6 us)
Async XLA Ops:
  7.2 10.1 %copy-start.1 = (bf16[2,64,2048]{2,1,0:T(8,128)(2,1)S(1)}, bf16[2,64,2048]{2,1,0:T(8,128)(2,1)}, u32[]{:S(2)}) copy-start(bf16[2,64,2048]{2,1,0:T(8,128)(2,1)} %param.11) | copy-start | bytes 1572868
  7.2 26.1 %copy-start.2 = (bf16[2,64,2048]{2,1,0:T(8,128)(2,1)S(1)}, bf16[2,64,2048]{2,1,0:T(8,128)(2,1)}, u32[]{:S(2)}) copy-start(bf16[2,64,2048]{2,1,0:T(8,128)(2,1)} %param.13) | copy-start | bytes 1572868
  11.1 18.5 %all-to-all-start = ((bf16[16,2,8192]{2,1,0:T(2,128)(2,1)}), bf16[16,2,8192]{2,1,0:T(2,128)(2,1)S(1)}, u32[]{:S(2)}, u32[]{:S(2)}) async-start(bf16[16,2,8192]{2,1,0:T(2,128)(2,1)} %reshape.222), calls=%async_computation | async-start | bytes 1048576 | tf_op jit(solution)/shard_map/all_to_all | solution.py:130
  29.7 15.9 %all-to-all-start.1 = ((bf16[16,2,8192]{2,1,0:T(2,128)(2,1)}), bf16[16,2,8192]{2,1,0:T(2,128)(2,1)S(1)}, u32[]{:S(2)}, u32[]{:S(2)}) async-start(bf16[16,2,8192]{2,1,0:T(2,128)(2,1)} %reshape.224), calls=%async_computation.1 | async-start | bytes 1048576 | tf_op jit(solution)/shard_map/all_to_all | solution.py:129
  45.6 15.9 %all-to-all-start.2 = ((bf16[16,2,8192]{2,1,0:T(2,128)(2,1)}), bf16[16,2,8192]{2,1,0:T(2,128)(2,1)S(1)}, u32[]{:S(2)}, u32[]{:S(2)}) async-start(bf16[16,2,8192]{2,1,0:T(2,128)(2,1)} %reshape.226), calls=%async_computation.2 | async-start | bytes 1048576 | tf_op jit(solution)/shard_map/all_to_all | solution.py:131
  67.9 18.3 %copy-start.3 = (f32[7,2048]{1,0:T(8,128)S(1)}, f32[7,2048]{1,0:T(8,128)}, u32[]{:S(2)}) copy-start(f32[7,2048]{1,0:T(8,128)} %param.15) | copy-start | bytes 172036
  67.9 21.2 %copy-start.5 = (f32[2048]{0:T(1024)S(1)}, f32[2048]{0:T(1024)}, u32[]{:S(2)}) copy-start(f32[2048]{0:T(1024)} %param.16) | copy-start | bytes 24580
  83.5 2.7 collective-permute-start
  84.8 4.1 %collective-permute-start.1 = (bf16[2,3,2048]{2,1,0:T(4,128)(2,1)S(1)}, bf16[2,3,2048]{2,1,0:T(4,128)(2,1)S(1)}, u32[]{:S(2)}, u32[]{:S(2)}) collective-permute-start(bf16[2,3,2048]{2,1,0:T(4,128)(2,1)S(1)} %get-tuple-element.148), channel_id=1, source_target_pairs={{1,0},{2,1},{3,2},{4,3},{5,4},{6,5},{7,6},{8,7},{9,8},{10,9},{11,1... | collective-permute-start | bytes 73736 | tf_op jit(solution)/shard_map/ppermute | solution.py:19
  89.1 1.2 copy-start
  89.1 1.2 copy-start.4
  92.0 8.2 %collective-permute-start.2 = (f32[2,3,2048]{2,1,0:T(4,128)S(1)}, f32[2,3,2048]{2,1,0:T(4,128)S(1)}, u32[]{:S(2)}, u32[]{:S(2)}) collective-permute-start(f32[2,3,2048]{2,1,0:T(4,128)S(1)} %get-tuple-element.145), channel_id=1, source_target_pairs={{1,0},{2,1},{3,2},{4,3},{5,4},{6,5},{7,6},{8,7},{9,8},{10,9},{11,1... | collective-permute-start | bytes 147464 | tf_op jit(solution)/shard_map/ppermute | solution.py:19
  93.3 7.6 %collective-permute-start.3 = (f32[2,3,2048]{2,1,0:T(4,128)S(1)}, f32[2,3,2048]{2,1,0:T(4,128)S(1)}, u32[]{:S(2)}, u32[]{:S(2)}) collective-permute-start(f32[2,3,2048]{2,1,0:T(4,128)S(1)} %get-tuple-element.146), channel_id=1, source_target_pairs={{0,1},{1,2},{2,3},{3,4},{4,5},{5,6},{6,7},{7,8},{8,9},{9,10},{10,1... | collective-permute-start | bytes 147464 | tf_op jit(solution)/shard_map/ppermute | solution.py:16
  141.2 37.5 %copy-start.6 = (u32[256]{0:T(256)S(1)}, u32[256]{0:T(256)}, u32[]{:S(2)}) copy-start(u32[256]{0:T(256)} %constant.57) | copy-start | bytes 3076
  143.2 15.9 %all-to-all-start.7 = ((bf16[2,1024,128]{2,0,1:T(2,128)(2,1)}), bf16[2,1024,128]{2,0,1:T(2,128)(2,1)S(1)}, u32[]{:S(2)}, u32[]{:S(2)}) async-start(bf16[2,1024,128]{2,0,1:T(2,128)(2,1)} %copy.58), calls=%async_computation.7 | async-start | bytes 1048576 | tf_op jit(solution)/shard_map/all_to_all | solution.py:166
  159.1 15.9 %all-to-all-start.6 = ((bf16[2,1024,128]{2,0,1:T(2,128)(2,1)}), bf16[2,1024,128]{2,0,1:T(2,128)(2,1)S(1)}, u32[]{:S(2)}, u32[]{:S(2)}) async-start(bf16[2,1024,128]{2,0,1:T(2,128)(2,1)} %copy.55), calls=%async_computation.6 | async-start | bytes 1048576 | tf_op jit(solution)/shard_map/all_to_all | solution.py:165
  175.0 123.8 %all-to-all-start.5 = ((bf16[2,1024,128]{2,0,1:T(2,128)(2,1)}), bf16[2,1024,128]{2,0,1:T(2,128)(2,1)S(1)}, u32[]{:S(2)}, u32[]{:S(2)}) async-start(bf16[2,1024,128]{2,0,1:T(2,128)(2,1)} %copy.52), calls=%async_computation.5 | async-start | bytes 1048576 | tf_op jit(solution)/shard_map/all_to_all | solution.py:164
  178.6 81.8 %reduce-scatter.4.cloned.1.call-start = ((), (), s32[]{:S(2)}) async-start(), calls=%async_computation.9 | async-start | bytes 557056
Sparse Core Ops, SparseCore 0:
  184.0 76.3 reduce-scatter.3
where the time goes:
time: 308 us; the launch traced here: 307 us
  blocking collectives  113 us (37%)
  waiting for transfers between devices  95.6 us (31%)
  starting transfers between devices  34.8 us (11%)
  local copies, waits for them, and re-layouts  27.3 us (9%)
  between operations  15.2 us (5%)
  matrix products  12.6 us (4%)
  other arithmetic  7.88 us (3%)
    unnamed x2, waiting for transfers between devices  40.2 us
    unnamed x1, blocking collectives  38.9 us
    psum x1, blocking collectives, per_device(): lax.psum((weight_part, bias_part, gain_part), 'dp')  35.7 us
    all_to_all x1, blocking collectives, per_device(): lax.all_to_all(grad_frames, 'seq', split_axis=2, concat_axis=1, tiled=True)  23.7 us
    all_to_all x1, blocking collectives, per_device(): lax.all_to_all(attended, 'seq', split_axis=1, concat_axis=2, tiled=True)  15 us
    unnamed x28, local copies, waits for them, and re-layouts  14.3 us
    all_to_all x1, waiting for transfers between devices, per_device(): lax.all_to_all(value_part, 'seq', split_axis=1, concat_axis=2, tiled=True)  11.2 us
    all_to_all x1, waiting for transfers between devices, per_device(): lax.all_to_all(key_part, 'seq', split_axis=1, concat_axis=2, tiled=True)  11.2 us
  transfers between devices with their start and end apart: 11, of which 8 were waited for; matrix products, arithmetic and copies ran while one was open for 5% of the time, Pallas kernels for 0%

commit v1 on v0

v1 whole, which is shorter than its diff:
```python
import functools
import math

import jax
import jax.numpy as jnp
from jax import lax
from jax.experimental import pallas as pl
from jax.experimental.pallas import tpu as pltpu
from jax.sharding import PartitionSpec as P

HDIM = 128
SUB = 8
HEADS = 2
TAPS = 7
HALF = TAPS // 2
ROWS = 16
BLOCK = 256
LIMIT = 56 * 1024 * 1024
EPS = 1e-06

NT = (((1,), (1,)), ((), ()))
TN = (((0,), (0,)), ((), ()))


def dot(a, b, dims=(((1,), (0,)), ((), ()))):
    return lax.dot_general(a, b, dims, preferred_element_type=jnp.float32)


def pack_kernel(*refs):
    *sources, packed = refs
    for a, ref in enumerate(sources):
        for x in range(2):
            for core in range(2):
                for hh in range(HEADS):
                    lane = (hh * 2 + core) * HDIM
                    packed[x * 2 + core, a, hh] = ref[x, :, lane : lane + HDIM]


def unpack_kernel(packed, *results):
    for a, ref in enumerate(results):
        for x in range(2):
            for core in range(2):
                for hh in range(HEADS):
                    lane = (hh * 2 + core) * HDIM
                    ref[x, :, lane : lane + HDIM] = packed[x * 2 + core, a, hh]


def pack(arrays, seq):
    count = len(arrays)
    _, frames, width = arrays[0].shape
    steps = seq // 4
    return pl.pallas_call(
        pack_kernel,
        grid=(steps,),
        in_specs=[pl.BlockSpec((2, frames, width // steps), lambda i: (0, 0, i))] * count,
        out_specs=pl.BlockSpec((4, count, HEADS, frames, HDIM), lambda i: (i, 0, 0, 0, 0)),
        out_shape=jax.ShapeDtypeStruct((seq, count, HEADS, frames, HDIM), arrays[0].dtype),
        compiler_params=pltpu.CompilerParams(vmem_limit_bytes=LIMIT),
        name="pack",
    )(*arrays)


def unpack(packed, width):
    seq, count, _, frames, _ = packed.shape
    steps = seq // 4
    return pl.pallas_call(
        unpack_kernel,
        grid=(steps,),
        in_specs=[pl.BlockSpec((4, count, HEADS, frames, HDIM), lambda i: (i, 0, 0, 0, 0))],
        out_specs=[pl.BlockSpec((2, frames, width // steps), lambda i: (0, 0, i))] * count,
        out_shape=[jax.ShapeDtypeStruct((2, frames, width), packed.dtype)] * count,
        compiler_params=pltpu.CompilerParams(vmem_limit_bytes=LIMIT),
        name="unpack",
    )(packed)


def shifted_ends(padded, h, groups):
    sublane = lax.broadcasted_iota(jnp.int32, (SUB, HDIM), 0)
    for j in range(HALF):
        last = padded[h, (groups + j) * SUB : (groups + j + 1) * SUB, :]
        padded[h, j * SUB : (j + 1) * SUB, :] = jnp.where(
            sublane == 0, 0.0, pltpu.roll(last, 1, axis=0)
        )
    for j in range(HALF):
        first = padded[h, (HALF + j) * SUB : (HALF + j + 1) * SUB, :]
        padded[h, (HALF + groups + j) * SUB : (HALF + groups + j + 1) * SUB, :] = jnp.where(
            sublane == SUB - 1, 0.0, pltpu.roll(first, SUB - 1, axis=0)
        )


def forward_kernel(peers, recv, params, exps, outs, invs, att, conv, upper, stats):
    seq, _, _, frames, _ = recv.shape
    length = seq * frames
    groups = length // SUB
    scale = math.log2(math.e) / math.sqrt(HDIM)
    per_block = BLOCK // frames
    for h in range(HEADS):
        key = recv[:, 1, h].reshape(length, HDIM)
        value = recv[:, 2, h].reshape(length, HDIM)
        wide = jnp.concatenate([value, jnp.ones_like(value)], axis=1)
        for b in range(length // BLOCK):
            rows = slice(b * BLOCK, (b + 1) * BLOCK)
            query = recv[b * per_block : (b + 1) * per_block, 0, h].reshape(BLOCK, HDIM)
            scores = dot(query, key, NT)
            top = jnp.max(scores, axis=-1, keepdims=True)
            weights = jnp.exp2((scores - top) * scale).astype(jnp.bfloat16)
            exps[h, rows, :] = weights
            sums = dot(weights, wide)
            inv = 1.0 / sums[:, HDIM:]
            out = sums[:, :HDIM] * inv
            outs[h, rows, :] = out
            invs[h, rows, :] = inv
            rounded = out.astype(jnp.bfloat16).astype(jnp.float32)
            for j in range(BLOCK // groups):
                s = b * (BLOCK // groups) + j
                att[h, pl.ds(HALF * SUB + s, groups, stride=SUB), :] = rounded[
                    j * groups : (j + 1) * groups
                ]
        grad = recv[:, 3, h].reshape(length, HDIM).astype(jnp.float32)
        for s in range(SUB):
            upper[h, pl.ds(s, groups, stride=SUB), :] = grad[s * groups : (s + 1) * groups]
        shifted_ends(att, h, groups)

    lane = lax.broadcasted_iota(jnp.int32, (SUB, HDIM), 1)
    step = 16

    def some(i, carry):
        sumsq, dots = carry
        base = pl.multiple_of(i * step * SUB, step * SUB)
        total_sq = jnp.zeros((step * SUB, HDIM), jnp.float32)
        total_dot = jnp.zeros((step * SUB, HDIM), jnp.float32)
        for h in range(HEADS):
            par = params[h]
            value = par[TAPS][None, :]
            for t in range(TAPS):
                value = value + par[t][None, :] * att[h, pl.ds(base + t * SUB, step * SUB), :]
            conv[h, pl.ds(base, step * SUB), :] = value
            total_sq = total_sq + value * value
            total_dot = total_dot + value * (
                par[TAPS + 1][None, :] * upper[h, pl.ds(base, step * SUB), :]
            )
        sq = jnp.sum(total_sq, axis=-1, keepdims=True)
        dt = jnp.sum(total_dot, axis=-1, keepdims=True)
        for j in range(step):
            here = lane == i * step + j
            sumsq = jnp.where(here, sq[j * SUB : (j + 1) * SUB], sumsq)
            dots = jnp.where(here, dt[j * SUB : (j + 1) * SUB], dots)
        return sumsq, dots

    zero = jnp.zeros((SUB, HDIM), jnp.float32)
    sumsq, dots = lax.fori_loop(0, groups // step, some, (zero, zero))
    for p in range(peers):
        stats[p, :SUB, :] = sumsq
        stats[p, SUB:, :] = dots


def backward_kernel(
    width, stats, recv, params, exps, outs, invs, att, conv, upper, packed, part, cgrad, agrad, nat, sgrad
):
    seq, _, _, frames, _ = recv.shape
    length = seq * frames
    groups = length // SUB
    scale = 1.0 / math.sqrt(HDIM)
    total = jnp.sum(stats[...], axis=0)
    ratio = lax.rsqrt(total[:SUB] / width + EPS)
    beta = ratio * ratio * ratio * (total[SUB:] / width)
    zero = jnp.zeros((SUB, HDIM), jnp.float32)
    bias_sum, gain_sum = [zero] * HEADS, [zero] * HEADS
    gains = [jnp.broadcast_to(params[h, TAPS + 1][None, :], (SUB, HDIM)) for h in range(HEADS)]
    for r in range(groups):
        own = slice(r * SUB, (r + 1) * SUB)
        ratio_r = jnp.broadcast_to(ratio[:, r : r + 1], (SUB, HDIM))
        beta_r = jnp.broadcast_to(beta[:, r : r + 1], (SUB, HDIM))
        for h in range(HEADS):
            value, up = conv[h, own, :], upper[h, own, :]
            scaled = ratio_r * up
            grad = gains[h] * scaled - value * beta_r
            gain_sum[h] = gain_sum[h] + scaled * value
            bias_sum[h] = bias_sum[h] + grad
            cgrad[h, (HALF + r) * SUB : (HALF + r + 1) * SUB, :] = grad
    step = 8
    for h in range(HEADS):
        shifted_ends(cgrad, h, groups)
        par = params[h]

        def some(i, carry):
            base = pl.multiple_of(i * step * SUB, step * SUB)
            back = upper[h, pl.ds(base, step * SUB), :]
            own = cgrad[h, pl.ds(base + HALF * SUB, step * SUB), :]
            sums = []
            for t in range(TAPS):
                back = back + par[t][None, :] * cgrad[
                    h, pl.ds(base + (2 * HALF - t) * SUB, step * SUB), :
                ]
                term = own * att[h, pl.ds(base + t * SUB, step * SUB), :]
                sums.append(carry[t] + jnp.sum(term.reshape(step, SUB, HDIM), axis=0))
            agrad[pl.ds(base, step * SUB), :] = back
            return tuple(sums)

        taps = lax.fori_loop(0, groups // step, some, (zero,) * TAPS)
        for t in range(TAPS):
            part[h, t : t + 1, :] = jnp.sum(taps[t], axis=0, keepdims=True)
        part[h, TAPS : TAPS + 1, :] = jnp.sum(bias_sum[h], axis=0, keepdims=True)
        part[h, TAPS + 1 : TAPS + 2, :] = jnp.sum(gain_sum[h], axis=0, keepdims=True)
        part[h, TAPS + 2 :, :] = jnp.zeros((ROWS - TAPS - 2, HDIM), jnp.float32)
        for s in range(SUB):
            nat[s * groups : (s + 1) * groups, :] = agrad[pl.ds(s, groups, stride=SUB), :].astype(
                jnp.bfloat16
            )

        query = recv[:, 0, h].reshape(length, HDIM)
        key = recv[:, 1, h].reshape(length, HDIM)
        value = recv[:, 2, h].reshape(length, HDIM)
        inv = invs[h]
        per_block = BLOCK // frames
        for b in range(length // BLOCK):
            rows = slice(b * BLOCK, (b + 1) * BLOCK)
            grad = nat[rows, :]
            prob_grad = dot(grad, value, NT)
            delta = jnp.sum(grad.astype(jnp.float32) * outs[h, rows, :], axis=-1, keepdims=True)
            score_grad = (exps[h, rows, :].astype(jnp.float32) * (prob_grad - delta)).astype(
                jnp.bfloat16
            )
            sgrad[rows, :] = score_grad
            result = dot(score_grad, key) * (inv[rows] * scale)
            packed[b * per_block : (b + 1) * per_block, 0, h] = result.astype(jnp.bfloat16).reshape(
                per_block, frames, HDIM
            )
        scaled_query = (query.astype(jnp.float32) * inv).astype(jnp.bfloat16)
        key_grad = dot(sgrad[...], scaled_query, TN) * scale
        packed[:, 1, h] = key_grad.astype(jnp.bfloat16).reshape(seq, frames, HDIM)
        scaled_grad = (nat[...].astype(jnp.float32) * inv).astype(jnp.bfloat16)
        value_grad = dot(exps[h], scaled_grad, TN)
        packed[:, 2, h] = value_grad.astype(jnp.bfloat16).reshape(seq, frames, HDIM)


def in_vmem(shape, dtype):
    return pltpu.VMEM(shape, dtype)


def held(count):
    return [pl.BlockSpec(memory_space=pltpu.VMEM)] * count


def forward(recv, params, peers):
    seq, _, _, frames, _ = recv.shape
    length = seq * frames
    shapes = [
        ((HEADS, length, length), jnp.bfloat16),
        ((HEADS, length, HDIM), jnp.float32),
        ((HEADS, length, HDIM), jnp.float32),
        ((HEADS, length + 2 * HALF * SUB, HDIM), jnp.float32),
        ((HEADS, length, HDIM), jnp.float32),
        ((HEADS, length, HDIM), jnp.float32),
        ((peers, 2 * SUB, HDIM), jnp.float32),
    ]
    return pl.pallas_call(
        functools.partial(forward_kernel, peers),
        in_specs=held(2),
        out_specs=held(len(shapes)),
        out_shape=[jax.ShapeDtypeStruct(*s) for s in shapes],
        compiler_params=pltpu.CompilerParams(vmem_limit_bytes=LIMIT),
        name="forward",
    )(recv, params)


def backward(width, stats, recv, params, saved):
    seq, _, _, frames, _ = recv.shape
    length = seq * frames
    return pl.pallas_call(
        functools.partial(backward_kernel, width),
        in_specs=held(3 + len(saved)),
        out_specs=held(2),
        out_shape=[
            jax.ShapeDtypeStruct((seq, 3, HEADS, frames, HDIM), jnp.bfloat16),
            jax.ShapeDtypeStruct((HEADS, ROWS, HDIM), jnp.float32),
        ],
        scratch_shapes=[
            pltpu.VMEM((HEADS, length + 2 * HALF * SUB, HDIM), jnp.float32),
            pltpu.VMEM((length, HDIM), jnp.float32),
            pltpu.VMEM((length, HDIM), jnp.bfloat16),
            pltpu.VMEM((length, length), jnp.bfloat16),
        ],
        compiler_params=pltpu.CompilerParams(vmem_limit_bytes=LIMIT),
        name="backward",
    )(stats, recv, params, *saved)


def exchange(x, groups=None):
    return lax.all_to_all(
        x, "seq", split_axis=0, concat_axis=0, tiled=True, axis_index_groups=groups
    )


def own_params(conv_weight, conv_bias, gain, y, core):
    rows = jnp.concatenate([conv_weight, conv_bias[None], gain[None]], axis=0)
    rows = jnp.pad(rows, ((0, ROWS - rows.shape[0]), (0, 0)))
    rows = rows.reshape(ROWS, -1, HEADS, 2, HDIM)
    rows = lax.dynamic_index_in_dim(rows, y, axis=1, keepdims=False)
    rows = lax.dynamic_index_in_dim(rows, core, axis=2, keepdims=False)
    return rows.transpose(1, 0, 2)


def sum_params(part, x, seq, dp):
    own = lax.dynamic_index_in_dim(part, x, axis=0, keepdims=False)
    other = lax.dynamic_index_in_dim(part, 1 - x, axis=0, keepdims=False)
    total = own + lax.ppermute(other, "seq", [(i, i ^ 2) for i in range(seq)])
    shift = dp // 2
    shifts = [shift] + [1 << i for i in range(shift.bit_length() - 1)]
    for shift in shifts:
        total = total + lax.ppermute(total, "dp", [(i, i ^ shift) for i in range(dp)])
    return total


def per_device(queries, keys, values, out_grad, conv_weight, conv_bias, gain):
    width = queries.shape[2]
    seq, dp = lax.axis_size("seq"), lax.axis_size("dp")
    index = lax.axis_index("seq")
    y, x, core = index // 4, (index // 2) % 2, index % 2
    same_x = [[b * 4 + a * 2 + c for b in range(seq // 4) for c in range(2)] for a in range(2)]
    params = own_params(conv_weight, conv_bias, gain, y, core)
    recv = exchange(pack((queries, keys, values, out_grad), seq))
    *saved, stats = forward(recv, params, len(same_x[0]))
    stats = exchange(stats, same_x)
    packed, part = backward(width, stats, recv, params, saved)
    total = sum_params(part, x, seq, dp)
    query_grad, key_grad, value_grad = unpack(exchange(packed), width)
    return (query_grad, key_grad, value_grad, total[:TAPS], total[TAPS], total[TAPS + 1])


def solution(mesh):
    frames = P("dp", "seq", None)
    return jax.shard_map(
        per_device,
        mesh=mesh,
        in_specs=(frames, frames, frames, frames, P(), P(), P()),
        out_specs=(frames, frames, frames, P(None, "seq"), P("seq"), P("seq")),
        check_vma=False,
    )
```

time: 308 us -> 127 us (0.41)
  blocking collectives: 113 us -> 9.57 us
  waiting for transfers between devices: 95.6 us -> 56.6 us
  Pallas kernels: 0 us -> 29.9 us
  local copies, waits for them, and re-layouts: 27.3 us -> 4.42 us
  between operations: 15.2 us -> 0.8 us
  matrix products: 12.6 us -> 0 us
  starting transfers between devices: 34.8 us -> 25.5 us
  other arithmetic: 7.88 us -> 0.05 us
    unnamed x2 -> x0, waiting for transfers between devices: 40.2 us -> none
    unnamed x1 -> x0, blocking collectives: 38.9 us -> none
    psum x1 -> x0, blocking collectives: 35.7 us -> none  [per_device(): lax.psum((weight_part, bias_part, gain_part), 'dp')]
    pallas_call x0 -> x4, Pallas kernels: none -> 29.9 us  [the longest x1 12.4 us: backward(): pl.pallas_call(functools.partial(backward_kernel, width), in_specs=held(3...]
    all_to_all x2 -> x1, blocking collectives: 38.7 us -> 9.57 us  [exchange(): lax.all_to_all(x, 'seq', split_axis=0, concat_axis=0, tiled=True, axis_in...]
    ppermute x4 -> x5, waiting for transfers between devices: 3.42 us -> 27.9 us  [the longest x1 19.3 us: sum_params(): total = own + lax.ppermute(other, 'seq', [(i, i ^ 2) for i in range(seq)])]
    all_to_all x6 -> x2, waiting for transfers between devices: 52 us -> 28.7 us  [exchange(): lax.all_to_all(x, 'seq', split_axis=0, concat_axis=0, tiled=True, axis_in...]
    all_to_all x6 -> x2, starting transfers between devices: 24 us -> 10.1 us  [exchange(): lax.all_to_all(x, 'seq', split_axis=0, concat_axis=0, tiled=True, axis_in...]
  transfers between devices with their start and end apart: 11 -> 7, of which waited for: 8 -> 6; matrix products, arithmetic and copies ran while one was open for 5% -> 2% of each run, Pallas kernels for 0% -> 0%
where the time goes in v1:
time: 127 us
  waiting for transfers between devices  56.6 us (45%)
  Pallas kernels  29.9 us (24%)
  starting transfers between devices  25.5 us (20%)
  blocking collectives  9.57 us (8%)
  local copies, waits for them, and re-layouts  4.42 us (3%)
    all_to_all x2, waiting for transfers between devices, exchange(): lax.all_to_all(x, 'seq', split_axis=0, concat_axis=0, tiled=True, axis_in...  28.7 us
    ppermute x1, waiting for transfers between devices, sum_params(): total = own + lax.ppermute(other, 'seq', [(i, i ^ 2) for i in range(seq)])  19.3 us
    pallas_call x1, Pallas kernels, backward(): pl.pallas_call(functools.partial(backward_kernel, width), in_specs=held(3...  12.4 us
    ppermute x4, starting transfers between devices, sum_params(): lax.ppermute(total, 'dp', [(i, i ^ shift) for i in range(dp)])  12.1 us
    all_to_all x2, starting transfers between devices, exchange(): lax.all_to_all(x, 'seq', split_axis=0, concat_axis=0, tiled=True, axis_in...  10.1 us
    pallas_call x1, Pallas kernels, forward(): pl.pallas_call(functools.partial(forward_kernel, peers), in_specs=held(2)...  9.89 us
    all_to_all x1, blocking collectives, exchange(): lax.all_to_all(x, 'seq', split_axis=0, concat_axis=0, tiled=True, axis_in...  9.57 us
    ppermute x4, waiting for transfers between devices, sum_params(): lax.ppermute(total, 'dp', [(i, i ^ shift) for i in range(dp)])  8.61 us
  transfers between devices with their start and end apart: 7, of which 6 were waited for; matrix products, arithmetic and copies ran while one was open for 2% of the time, Pallas kernels for 0%

profile of v1, /device:TPU:2, one launch (start us, length us, event | category | flops | bytes accessed | tf_op | source)
XLA Modules:
  0.0 126.9 jit_solution(15242301997001881006)
XLA Ops:
  0.6 4.0 %pack.1 = bf16[16,4,2,64,128]{4,3,2,1,0:T(8,128)(2,1)} custom-call(bf16[2,64,2048]{2,1,0:T(8,128)(2,1)} %refs_0_.1, bf16[2,64,2048]{2,1,0:T(8,128)(2,1)} %refs_1_.1, bf16[2,64,2048]{2,1,0:T(8,128)(2,1)} %refs_2_.1, bf16[2,64,2048]{2,1,0:T(8,128)(2,1)} %refs_3_.1), custom_call_target="tpu_custom_call" | custom-call | tf_op jit(solution)/shard_map/pack/pallas_call | solution.py:52
  4.6 6.3 %all-to-all-start = ((bf16[16,4,2,64,128]{4,3,2,1,0:T(8,128)(2,1)}), bf16[16,4,2,64,128]{4,3,2,1,0:T(8,128)(2,1)S(1)}, u32[]{:S(2)}, u32[]{:S(2)}) async-start(bf16[16,4,2,64,128]{4,3,2,1,0:T(8,128)(2,1)} %pack.1), calls=%async_computation | async-start | bytes 4194304 | tf_op jit(solution)/shard_map/all_to_all | solution.py:290
  11.0 0.1 reshape.17
  11.2 0.6 copy.16
  11.8 28.7 %all-to-all-done.recv = bf16[16,4,2,64,128]{4,3,2,1,0:T(8,128)(2,1)S(1)} async-done(((bf16[16,4,2,64,128]{4,3,2,1,0:T(8,128)(2,1)}), bf16[16,4,2,64,128]{4,3,2,1,0:T(8,128)(2,1)S(1)}, u32[]{:S(2)}, u32[]{:S(2)}) %all-to-all-start) | async-done | bytes 2097184 | tf_op jit(solution)/shard_map/all_to_all | solution.py:290
  40.5 1.4 %copy-done = bf16[16,4,2,64,128]{4,3,2,1,0:T(8,128)(2,1)} copy-done((bf16[16,4,2,64,128]{4,3,2,1,0:T(8,128)(2,1)}, bf16[16,4,2,64,128]{4,3,2,1,0:T(8,128)(2,1)S(1)}, u32[]{:S(2)}) %copy-start) | copy-done | bytes 2097176
  41.9 9.9 %forward.1 = (bf16[2,1024,1024]{2,1,0:T(8,128)(2,1)}, f32[2,1024,128]{2,1,0:T(8,128)}, f32[2,1024,128]{2,1,0:T(8,128)}, f32[2,1072,128]{2,1,0:T(8,128)}, f32[2,1...) custom-call(bf16[16,4,2,64,128]{4,3,2,1,0:T(8,128)(2,1)} %copy-done, f32[2,16,128]{2,1,0:T(8,128)} %bitcast.15), custom_call_target="tpu_custom_call" | custom-call | tf_op jit(solution)/shard_map/forward/pallas_call | solution.py:257
  51.7 9.6 %all_to_all.15.stats = f32[8,16,128]{2,1,0:T(8,128)} all-to-all(f32[8,16,128]{2,1,0:T(8,128)} %get-tuple-element.18), channel_id=1, replica_groups={{0,1,4,5,8,9,12,13},{2,3,6,7,10,11,14,15},{16,17,20,21,24,25,28,29},{18..., dimensions={0} | all-to-all | bytes 131072 | tf_op jit(solution)/shard_map/all_to_all | solution.py:290
  61.3 12.4 %backward.1 = (bf16[16,3,2,64,128]{4,3,2,1,0:T(8,128)(2,1)}, f32[2,16,128]{2,1,0:T(8,128)}) custom-call(f32[8,16,128]{2,1,0:T(8,128)} %all_to_all.15.stats, bf16[16,4,2,64,128]{4,3,2,1,0:T(8,128)(2,1)} %copy-done, f32[2,16,128]{2,1,0:T(8,128)} %bitcast.16, bf16[2,1024,1024]{2,1,0:T(8,128)(2,1)} %get-tuple-element.19.exps, ...), custom_call_target="tpu_custom_call" | custom-call | tf_op jit(solution)/shard_map/backward/pallas_call | solution.py:270
  73.7 3.8 %all-to-all-start.2 = ((bf16[16,3,2,64,128]{4,3,2,1,0:T(8,128)(2,1)}), bf16[16,3,2,64,128]{4,3,2,1,0:T(8,128)(2,1)S(1)}, u32[]{:S(2)}, u32[]{:S(2)}) async-start(bf16[16,3,2,64,128]{4,3,2,1,0:T(8,128)(2,1)} %get-tuple-element.25), calls=%async_computation.2 | async-start | bytes 3145728 | tf_op jit(solution)/shard_map/all_to_all | solution.py:290
  77.6 3.4 %collective-permute-start = (f32[16,128]{1,0:T(8,128)S(1)}, f32[16,128]{1,0:T(8,128)S(1)}, u32[]{:S(2)}, u32[]{:S(2)}) collective-permute-start(f32[16,128]{1,0:T(8,128)S(1)} %dynamic-slice_bitcast_fusion), channel_id=1, source_target_pairs={{0,2},{1,3},{2,0},{3,1},{4,6},{5,7},{6,4},{7,5},{8,10},{9,11},{10,... | collective-permute-start | bytes 24584 | tf_op jit(solution)/shard_map/ppermute | solution.py:307
  81.0 19.3 %collective-permute-done = f32[16,128]{1,0:T(8,128)S(1)} collective-permute-done((f32[16,128]{1,0:T(8,128)S(1)}, f32[16,128]{1,0:T(8,128)S(1)}, u32[]{:S(2)}, u32[]{:S(2)}) %collective-permute-start) | collective-permute-done | bytes 8224 | tf_op jit(solution)/shard_map/ppermute | solution.py:307
  100.3 0.0 collective-permute-start.1
  100.3 3.6 %collective-permute-done.1 = f32[16,128]{1,0:T(8,128)S(1)} collective-permute-done((f32[16,128]{1,0:T(8,128)S(1)}, f32[16,128]{1,0:T(8,128)S(1)}, u32[]{:S(2)}, u32[]{:S(2)}) %collective-permute-start.1) | collective-permute-done | bytes 8224 | tf_op jit(solution)/shard_map/ppermute | solution.py:311
  103.9 1.9 %collective-permute-start.2 = (f32[16,128]{1,0:T(8,128)S(1)}, f32[16,128]{1,0:T(8,128)S(1)}, u32[]{:S(2)}, u32[]{:S(2)}) collective-permute-start(f32[16,128]{1,0:T(8,128)S(1)} %add.54), channel_id=1, source_target_pairs={{0,16},{16,0},{32,48},{48,32},{64,80},{80,64},{96,112},{112,96},{1... | collective-permute-start | bytes 24584 | tf_op jit(solution)/shard_map/ppermute | solution.py:311
  105.9 1.7 %collective-permute-done.2 = f32[16,128]{1,0:T(8,128)S(1)} collective-permute-done((f32[16,128]{1,0:T(8,128)S(1)}, f32[16,128]{1,0:T(8,128)S(1)}, u32[]{:S(2)}, u32[]{:S(2)}) %collective-permute-start.2) | collective-permute-done | bytes 8224 | tf_op jit(solution)/shard_map/ppermute | solution.py:311
  107.6 3.3 %collective-permute-start.3 = (f32[16,128]{1,0:T(8,128)S(1)}, f32[16,128]{1,0:T(8,128)S(1)}, u32[]{:S(2)}, u32[]{:S(2)}) collective-permute-start(f32[16,128]{1,0:T(8,128)S(1)} %add.55), channel_id=1, source_target_pairs={{0,32},{16,48},{32,0},{48,16},{64,96},{80,112},{96,64},{112,80},{1... | collective-permute-start | bytes 24584 | tf_op jit(solution)/shard_map/ppermute | solution.py:311
  110.9 1.6 %collective-permute-done.3 = f32[16,128]{1,0:T(8,128)S(1)} collective-permute-done((f32[16,128]{1,0:T(8,128)S(1)}, f32[16,128]{1,0:T(8,128)S(1)}, u32[]{:S(2)}, u32[]{:S(2)}) %collective-permute-start.3) | collective-permute-done | bytes 8224 | tf_op jit(solution)/shard_map/ppermute | solution.py:311
  112.5 6.8 %collective-permute-start.4 = (f32[16,128]{1,0:T(8,128)S(1)}, f32[16,128]{1,0:T(8,128)S(1)}, u32[]{:S(2)}, u32[]{:S(2)}) collective-permute-start(f32[16,128]{1,0:T(8,128)S(1)} %add.56), channel_id=1, source_target_pairs={{0,64},{16,80},{32,96},{48,112},{64,0},{80,16},{96,32},{112,48},{1... | collective-permute-start | bytes 24584 | tf_op jit(solution)/shard_map/ppermute | solution.py:311
  119.3 1.6 %collective-permute-done.4 = f32[16,128]{1,0:T(8,128)S(1)} collective-permute-done((f32[16,128]{1,0:T(8,128)S(1)}, f32[16,128]{1,0:T(8,128)S(1)}, u32[]{:S(2)}, u32[]{:S(2)}) %collective-permute-start.4) | collective-permute-done | bytes 8224 | tf_op jit(solution)/shard_map/ppermute | solution.py:311
  121.0 0.6 slice.12
  121.6 0.5 slice_bitcast_fusion
  122.1 1.2 copy-done.1
  123.3 3.6 %unpack.1 = (bf16[2,64,2048]{2,1,0:T(8,128)(2,1)}, bf16[2,64,2048]{2,1,0:T(8,128)(2,1)}, bf16[2,64,2048]{2,1,0:T(8,128)(2,1)}) custom-call(bf16[16,3,2,64,128]{4,3,2,1,0:T(8,128)(2,1)} %copy-done.1), custom_call_target="tpu_custom_call" | custom-call | tf_op jit(solution)/shard_map/unpack/pallas_call | solution.py:66
  (19 shorter events, 0.1 us)
Async XLA Ops:
  4.6 6.3 %copy-start.2 = (f32[7,2048]{1,0:T(8,128)S(1)}, f32[7,2048]{1,0:T(8,128)}, u32[]{:S(2)}) copy-start(f32[7,2048]{1,0:T(8,128)} %param.11) | copy-start | bytes 172036
  4.6 6.3 %copy-start.4 = (f32[2048]{0:T(1024)S(1)}, f32[2048]{0:T(1024)}, u32[]{:S(2)}) copy-start(f32[2048]{0:T(1024)} %param.13) | copy-start | bytes 24580
  4.6 6.4 %copy-start.5 = (f32[2048]{0:T(1024)S(1)}, f32[2048]{0:T(1024)}, u32[]{:S(2)}) copy-start(f32[2048]{0:T(1024)} %param.12) | copy-start | bytes 24580
  4.6 35.9 %all-to-all-start = ((bf16[16,4,2,64,128]{4,3,2,1,0:T(8,128)(2,1)}), bf16[16,4,2,64,128]{4,3,2,1,0:T(8,128)(2,1)S(1)}, u32[]{:S(2)}, u32[]{:S(2)}) async-start(bf16[16,4,2,64,128]{4,3,2,1,0:T(8,128)(2,1)} %pack.1), calls=%async_computation | async-start | bytes 4194304 | tf_op jit(solution)/shard_map/all_to_all | solution.py:290
  40.5 1.4 %copy-start = (bf16[16,4,2,64,128]{4,3,2,1,0:T(8,128)(2,1)}, bf16[16,4,2,64,128]{4,3,2,1,0:T(8,128)(2,1)S(1)}, u32[]{:S(2)}) copy-start(bf16[16,4,2,64,128]{4,3,2,1,0:T(8,128)(2,1)S(1)} %all-to-all-done.recv) | copy-start | bytes 6291460
  73.7 3.9 %copy-start.3 = (f32[2,16,128]{2,1,0:T(8,128)S(1)}, f32[2,16,128]{2,1,0:T(8,128)}, u32[]{:S(2)}) copy-start(f32[2,16,128]{2,1,0:T(8,128)} %get-tuple-element.29) | copy-start | bytes 49156
  73.7 48.4 %all-to-all-start.2 = ((bf16[16,3,2,64,128]{4,3,2,1,0:T(8,128)(2,1)}), bf16[16,3,2,64,128]{4,3,2,1,0:T(8,128)(2,1)S(1)}, u32[]{:S(2)}, u32[]{:S(2)}) async-start(bf16[16,3,2,64,128]{4,3,2,1,0:T(8,128)(2,1)} %get-tuple-element.25), calls=%async_computation.2 | async-start | bytes 3145728 | tf_op jit(solution)/shard_map/all_to_all | solution.py:290
  77.6 22.7 %collective-permute-start = (f32[16,128]{1,0:T(8,128)S(1)}, f32[16,128]{1,0:T(8,128)S(1)}, u32[]{:S(2)}, u32[]{:S(2)}) collective-permute-start(f32[16,128]{1,0:T(8,128)S(1)} %dynamic-slice_bitcast_fusion), channel_id=1, source_target_pairs={{0,2},{1,3},{2,0},{3,1},{4,6},{5,7},{6,4},{7,5},{8,10},{9,11},{10,... | collective-permute-start | bytes 24584 | tf_op jit(solution)/shard_map/ppermute | solution.py:307
  100.3 3.7 %collective-permute-start.1 = (f32[16,128]{1,0:T(8,128)S(1)}, f32[16,128]{1,0:T(8,128)S(1)}, u32[]{:S(2)}, u32[]{:S(2)}) collective-permute-start(f32[16,128]{1,0:T(8,128)S(1)} %bitcast_add_fusion), channel_id=1, source_target_pairs={{0,128},{16,144},{32,160},{48,176},{64,192},{80,208},{96,224},{112... | collective-permute-start | bytes 24584 | tf_op jit(solution)/shard_map/ppermute | solution.py:311
  103.9 3.7 %collective-permute-start.2 = (f32[16,128]{1,0:T(8,128)S(1)}, f32[16,128]{1,0:T(8,128)S(1)}, u32[]{:S(2)}, u32[]{:S(2)}) collective-permute-start(f32[16,128]{1,0:T(8,128)S(1)} %add.54), channel_id=1, source_target_pairs={{0,16},{16,0},{32,48},{48,32},{64,80},{80,64},{96,112},{112,96},{1... | collective-permute-start | bytes 24584 | tf_op jit(solution)/shard_map/ppermute | solution.py:311
  107.6 4.9 %collective-permute-start.3 = (f32[16,128]{1,0:T(8,128)S(1)}, f32[16,128]{1,0:T(8,128)S(1)}, u32[]{:S(2)}, u32[]{:S(2)}) collective-permute-start(f32[16,128]{1,0:T(8,128)S(1)} %add.55), channel_id=1, source_target_pairs={{0,32},{16,48},{32,0},{48,16},{64,96},{80,112},{96,64},{112,80},{1... | collective-permute-start | bytes 24584 | tf_op jit(solution)/shard_map/ppermute | solution.py:311
  112.5 8.5 %collective-permute-start.4 = (f32[16,128]{1,0:T(8,128)S(1)}, f32[16,128]{1,0:T(8,128)S(1)}, u32[]{:S(2)}, u32[]{:S(2)}) collective-permute-start(f32[16,128]{1,0:T(8,128)S(1)} %add.56), channel_id=1, source_target_pairs={{0,64},{16,80},{32,96},{48,112},{64,0},{80,16},{96,32},{112,48},{1... | collective-permute-start | bytes 24584 | tf_op jit(solution)/shard_map/ppermute | solution.py:311
  122.1 1.2 copy-start.1

commit v2 on v1

v2 whole, which is shorter than its diff:
```python
import functools
import math

import jax
import jax.numpy as jnp
from jax import lax
from jax.experimental import pallas as pl
from jax.experimental.pallas import tpu as pltpu
from jax.sharding import PartitionSpec as P

HDIM = 128
SUB = 8
HEADS = 2
TAPS = 7
HALF = TAPS // 2
ROWS = 16
BLOCK = 256
LIMIT = 24 * 1024 * 1024
EPS = 1e-06

NT = (((1,), (1,)), ((), ()))
TN = (((0,), (0,)), ((), ()))


def dot(a, b, dims=(((1,), (0,)), ((), ()))):
    return lax.dot_general(a, b, dims, preferred_element_type=jnp.float32)


def pack_kernel(*refs):
    *sources, result, packed, sems, done = refs
    for y in range(packed.shape[0]):
        for a, ref in enumerate(sources):
            for core in range(2):
                for hh in range(HEADS):
                    lane = ((y * HEADS + hh) * 2 + core) * HDIM
                    pltpu.make_async_copy(
                        ref.at[:, :, lane : lane + HDIM], packed.at[y, :, core, a, hh], sems.at[y]
                    ).start()
    for y in range(packed.shape[0]):
        pltpu.make_async_copy(packed.at[y], packed.at[y], sems.at[y]).wait()
        pltpu.make_async_copy(packed.at[y], result.at[y], done).start()
    pltpu.make_async_copy(packed, result, done).wait()


def unpack_kernel(*refs):
    packed, *results, sem = refs
    for a, ref in enumerate(results):
        for y in range(packed.shape[0]):
            for core in range(2):
                for hh in range(HEADS):
                    lane = ((y * HEADS + hh) * 2 + core) * HDIM
                    pltpu.make_async_copy(
                        packed.at[y, :, core, a, hh], ref.at[:, :, lane : lane + HDIM], sem
                    ).start()
    pltpu.make_async_copy(packed, packed, sem).wait()


def pack(arrays, seq):
    count = len(arrays)
    _, frames, _ = arrays[0].shape
    packed = pl.pallas_call(
        pack_kernel,
        in_specs=[pl.BlockSpec(memory_space=pltpu.HBM)] * count,
        out_specs=pl.BlockSpec(memory_space=pltpu.HBM),
        out_shape=pltpu.HBM((seq // 4, 2, 2, count, HEADS, frames, HDIM), arrays[0].dtype),
        scratch_shapes=[
            pltpu.VMEM((seq // 4, 2, 2, count, HEADS, frames, HDIM), arrays[0].dtype),
            pltpu.SemaphoreType.DMA((seq // 4,)),
            pltpu.SemaphoreType.DMA,
        ],
        compiler_params=pltpu.CompilerParams(vmem_limit_bytes=LIMIT),
        name="pack",
    )(*[pltpu.with_memory_space_constraint(a, pltpu.HBM) for a in arrays])
    return packed.reshape(seq, count, HEADS, frames, HDIM)


def unpack(packed, width):
    seq, count, _, frames, _ = packed.shape
    return pl.pallas_call(
        unpack_kernel,
        in_specs=[pl.BlockSpec(memory_space=pltpu.VMEM)],
        out_specs=[pl.BlockSpec(memory_space=pltpu.HBM)] * count,
        out_shape=[pltpu.HBM((2, frames, width), packed.dtype)] * count,
        scratch_shapes=[pltpu.SemaphoreType.DMA],
        compiler_params=pltpu.CompilerParams(vmem_limit_bytes=LIMIT),
        name="unpack",
    )(*resident(packed.reshape(seq // 4, 2, 2, count, HEADS, frames, HDIM)))


def shifted_ends(padded, h, groups):
    sublane = lax.broadcasted_iota(jnp.int32, (SUB, HDIM), 0)
    for j in range(HALF):
        last = padded[h, (groups + j) * SUB : (groups + j + 1) * SUB, :]
        padded[h, j * SUB : (j + 1) * SUB, :] = jnp.where(
            sublane == 0, 0.0, pltpu.roll(last, 1, axis=0)
        )
    for j in range(HALF):
        first = padded[h, (HALF + j) * SUB : (HALF + j + 1) * SUB, :]
        padded[h, (HALF + groups + j) * SUB : (HALF + groups + j + 1) * SUB, :] = jnp.where(
            sublane == SUB - 1, 0.0, pltpu.roll(first, SUB - 1, axis=0)
        )


def turn(target, offset, natural):
    groups = natural.shape[0] // SUB
    for s in range(SUB):
        target[pl.ds(offset + s, groups, stride=SUB), :] = natural[s * groups : (s + 1) * groups]


def convolve(att, h, par, base, count):
    value = par[TAPS][None, :]
    for t in range(TAPS):
        value = value + par[t][None, :] * att[h, pl.ds(base + t * SUB, count), :]
    return value


def forward_kernel(
    peers, recv, params, exps_out, invs_out, outs, stats, exps, invs, upper, att, sems
):
    seq, _, _, frames, _ = recv.shape
    length = seq * frames
    groups = length // SUB
    scale = math.log2(math.e) / math.sqrt(HDIM)
    per_block = BLOCK // frames
    for h in range(HEADS):
        key = recv[:, 1, h].reshape(length, HDIM)
        value = recv[:, 2, h].reshape(length, HDIM)
        wide = jnp.concatenate([value, jnp.ones_like(value)], axis=1)
        for b in range(length // BLOCK):
            rows = slice(b * BLOCK, (b + 1) * BLOCK)
            query = recv[b * per_block : (b + 1) * per_block, 0, h].reshape(BLOCK, HDIM)
            scores = dot(query, key, NT)
            top = jnp.max(scores, axis=-1, keepdims=True)
            weights = jnp.exp2((scores - top) * scale).astype(jnp.bfloat16)
            exps[h, rows, :] = weights
            pltpu.make_async_copy(exps.at[h, rows], exps_out.at[h, rows], sems.at[0]).start()
            sums = dot(weights, wide)
            inv = 1.0 / sums[:, HDIM:]
            out = sums[:, :HDIM] * inv
            outs[h, rows, :] = out
            invs[h, rows, :] = inv
            rounded = out.astype(jnp.bfloat16).astype(jnp.float32)
            for j in range(BLOCK // groups):
                s = b * (BLOCK // groups) + j
                att[h, pl.ds(HALF * SUB + s, groups, stride=SUB), :] = rounded[
                    j * groups : (j + 1) * groups
                ]
        pltpu.make_async_copy(invs.at[h], invs_out.at[h], sems.at[1]).start()
        turn(upper.at[h], 0, recv[:, 3, h].reshape(length, HDIM).astype(jnp.float32))
        shifted_ends(att, h, groups)

    lane = lax.broadcasted_iota(jnp.int32, (SUB, HDIM), 1)
    step = 16

    def some(i, carry):
        sumsq, dots = carry
        base = pl.multiple_of(i * step * SUB, step * SUB)
        total_sq = jnp.zeros((step * SUB, HDIM), jnp.float32)
        total_dot = jnp.zeros((step * SUB, HDIM), jnp.float32)
        for h in range(HEADS):
            par = params[h]
            value = convolve(att, h, par, base, step * SUB)
            total_sq = total_sq + value * value
            total_dot = total_dot + value * (
                par[TAPS + 1][None, :] * upper[h, pl.ds(base, step * SUB), :]
            )
        sq = jnp.sum(total_sq, axis=-1, keepdims=True)
        dt = jnp.sum(total_dot, axis=-1, keepdims=True)
        for j in range(step):
            here = lane == i * step + j
            sumsq = jnp.where(here, sq[j * SUB : (j + 1) * SUB], sumsq)
            dots = jnp.where(here, dt[j * SUB : (j + 1) * SUB], dots)
        return sumsq, dots

    zero = jnp.zeros((SUB, HDIM), jnp.float32)
    sumsq, dots = lax.fori_loop(0, groups // step, some, (zero, zero))
    for p in range(peers):
        stats[p, :SUB, :] = sumsq
        stats[p, SUB:, :] = dots
    for i, (src, dst) in enumerate(((exps, exps_out), (invs, invs_out))):
        pltpu.make_async_copy(src, dst, sems.at[i]).wait()


def norm_kernel(
    width, stats, recv, params, outs, exps_in, invs_in, grads, part, exps, invs, cgrad, agrad, upper, att, sems
):
    seq, _, _, frames, _ = recv.shape
    length = seq * frames
    groups = length // SUB
    fetches = [
        pltpu.make_async_copy(invs_in, invs, sems.at[0]),
        pltpu.make_async_copy(exps_in.at[0], exps.at[0], sems.at[1]),
        pltpu.make_async_copy(exps_in.at[1], exps.at[1], sems.at[2]),
    ]
    for fetch in fetches:
        fetch.start()
    total = jnp.sum(stats[...], axis=0)
    ratio = lax.rsqrt(total[:SUB] / width + EPS)
    beta = ratio * ratio * ratio * (total[SUB:] / width)
    zero = jnp.zeros((SUB, HDIM), jnp.float32)
    bias_sum, gain_sum = [zero] * HEADS, [zero] * HEADS
    gains = [jnp.broadcast_to(params[h, TAPS + 1][None, :], (SUB, HDIM)) for h in range(HEADS)]
    for h in range(HEADS):
        turn(upper.at[h], 0, recv[:, 3, h].reshape(length, HDIM).astype(jnp.float32))
        turn(att.at[h], HALF * SUB, outs[h].astype(jnp.bfloat16).astype(jnp.float32))
        shifted_ends(att, h, groups)
    for r in range(groups):
        own = slice(r * SUB, (r + 1) * SUB)
        ratio_r = jnp.broadcast_to(ratio[:, r : r + 1], (SUB, HDIM))
        beta_r = jnp.broadcast_to(beta[:, r : r + 1], (SUB, HDIM))
        for h in range(HEADS):
            value, up = convolve(att, h, params[h], r * SUB, SUB), upper[h, own, :]
            scaled = ratio_r * up
            grad = gains[h] * scaled - value * beta_r
            gain_sum[h] = gain_sum[h] + scaled * value
            bias_sum[h] = bias_sum[h] + grad
            cgrad[h, (HALF + r) * SUB : (HALF + r + 1) * SUB, :] = grad
    step = 8
    for h in range(HEADS):
        shifted_ends(cgrad, h, groups)
        par = params[h]

        def some(i, carry):
            base = pl.multiple_of(i * step * SUB, step * SUB)
            back = upper[h, pl.ds(base, step * SUB), :]
            own = cgrad[h, pl.ds(base + HALF * SUB, step * SUB), :]
            sums = []
            for t in range(TAPS):
                back = back + par[t][None, :] * cgrad[
                    h, pl.ds(base + (2 * HALF - t) * SUB, step * SUB), :
                ]
                term = own * att[h, pl.ds(base + t * SUB, step * SUB), :]
                sums.append(carry[t] + jnp.sum(term.reshape(step, SUB, HDIM), axis=0))
            agrad[pl.ds(base, step * SUB), :] = back
            return tuple(sums)

        taps = lax.fori_loop(0, groups // step, some, (zero,) * TAPS)
        for t in range(TAPS):
            part[h, t : t + 1, :] = jnp.sum(taps[t], axis=0, keepdims=True)
        part[h, TAPS : TAPS + 1, :] = jnp.sum(bias_sum[h], axis=0, keepdims=True)
        part[h, TAPS + 1 : TAPS + 2, :] = jnp.sum(gain_sum[h], axis=0, keepdims=True)
        part[h, TAPS + 2 :, :] = jnp.zeros((ROWS - TAPS - 2, HDIM), jnp.float32)
        if h == 0:
            fetches[0].wait()
        for s in range(SUB):
            rows = slice(s * groups, (s + 1) * groups)
            grads[h, rows, :] = (agrad[pl.ds(s, groups, stride=SUB), :] * invs[h, rows, :]).astype(
                jnp.bfloat16
            )
    for fetch in fetches[1:]:
        fetch.wait()


def backward_kernel(recv, grads, exps, outs, packed_out, sgrad, packed, sent):
    seq, _, _, frames, _ = recv.shape
    length = seq * frames
    scale = 1.0 / math.sqrt(HDIM)
    per_block = BLOCK // frames
    for h in range(HEADS):
        query = recv[:, 0, h].reshape(length, HDIM)
        key = recv[:, 1, h].reshape(length, HDIM)
        value = recv[:, 2, h].reshape(length, HDIM)
        for b in range(length // BLOCK):
            rows = slice(b * BLOCK, (b + 1) * BLOCK)
            grad = grads[h, rows, :]
            prob_grad = dot(grad, value, NT)
            delta = jnp.sum(grad.astype(jnp.float32) * outs[h, rows, :], axis=-1, keepdims=True)
            score_grad = (exps[h, rows, :].astype(jnp.float32) * (prob_grad - delta)).astype(
                jnp.bfloat16
            )
            sgrad[rows, :] = score_grad
            result = dot(score_grad, key) * scale
            packed[0, h, b * per_block : (b + 1) * per_block] = result.astype(jnp.bfloat16).reshape(
                per_block, frames, HDIM
            )
        pltpu.make_async_copy(packed.at[0, h], packed_out.at[:, 0, h], sent).start()
        key_grad = dot(sgrad[...], query, TN) * scale
        packed[1, h] = key_grad.astype(jnp.bfloat16).reshape(seq, frames, HDIM)
        pltpu.make_async_copy(packed.at[1, h], packed_out.at[:, 1, h], sent).start()
        value_grad = dot(exps[h], grads[h], TN)
        packed[2, h] = value_grad.astype(jnp.bfloat16).reshape(seq, frames, HDIM)
        pltpu.make_async_copy(packed.at[2, h], packed_out.at[:, 2, h], sent).start()
    pltpu.make_async_copy(packed, packed, sent).wait()


def resident(*arrays):
    return [pltpu.with_memory_space_constraint(a, pltpu.VMEM) for a in arrays]


def held(count, space=pltpu.VMEM):
    return [pl.BlockSpec(memory_space=space)] * count


def forward(recv, params, peers):
    seq, _, _, frames, _ = recv.shape
    length = seq * frames
    exps = (HEADS, length, length), jnp.bfloat16
    rows = (HEADS, length, HDIM), jnp.float32
    return pl.pallas_call(
        functools.partial(forward_kernel, peers),
        in_specs=held(2),
        out_specs=held(2, pltpu.HBM) + held(2),
        out_shape=[
            pltpu.HBM(*exps),
            pltpu.HBM(*rows),
            pltpu.VMEM(*rows),
            pltpu.VMEM((peers, 2 * SUB, HDIM), jnp.float32),
        ],
        scratch_shapes=[
            pltpu.VMEM(*exps),
            pltpu.VMEM(*rows),
            pltpu.VMEM(*rows),
            pltpu.VMEM((HEADS, length + 2 * HALF * SUB, HDIM), jnp.float32),
            pltpu.SemaphoreType.DMA((2,)),
        ],
        compiler_params=pltpu.CompilerParams(vmem_limit_bytes=LIMIT),
        name="forward",
    )(*resident(recv, params))


def norm(width, stats, recv, params, outs, exps, invs):
    seq, _, _, frames, _ = recv.shape
    length = seq * frames
    padded = pltpu.VMEM((HEADS, length + 2 * HALF * SUB, HDIM), jnp.float32)
    return pl.pallas_call(
        functools.partial(norm_kernel, width),
        in_specs=held(4) + held(2, pltpu.HBM),
        out_specs=held(3),
        out_shape=[
            pltpu.VMEM((HEADS, length, HDIM), jnp.bfloat16),
            pltpu.VMEM((HEADS, ROWS, HDIM), jnp.float32),
            pltpu.VMEM(exps.shape, exps.dtype),
        ],
        scratch_shapes=[
            pltpu.VMEM(invs.shape, invs.dtype),
            padded,
            pltpu.VMEM((length, HDIM), jnp.float32),
            pltpu.VMEM((HEADS, length, HDIM), jnp.float32),
            padded,
            pltpu.SemaphoreType.DMA((3,)),
        ],
        compiler_params=pltpu.CompilerParams(vmem_limit_bytes=LIMIT),
        name="norm",
    )(
        *resident(stats, recv, params, outs),
        *[pltpu.with_memory_space_constraint(a, pltpu.HBM) for a in (exps, invs)],
    )


def backward(recv, grads, exps, outs):
    seq, _, _, frames, _ = recv.shape
    length = seq * frames
    return pl.pallas_call(
        backward_kernel,
        in_specs=held(4),
        out_specs=pl.BlockSpec(memory_space=pltpu.HBM),
        out_shape=pltpu.HBM((seq, 3, HEADS, frames, HDIM), jnp.bfloat16),
        scratch_shapes=[
            pltpu.VMEM((length, length), jnp.bfloat16),
            pltpu.VMEM((3, HEADS, seq, frames, HDIM), jnp.bfloat16),
            pltpu.SemaphoreType.DMA,
        ],
        compiler_params=pltpu.CompilerParams(vmem_limit_bytes=LIMIT),
        cost_estimate=pl.CostEstimate(
            flops=16 * HEADS * length * length * HDIM, bytes_accessed=1 << 24, transcendentals=0
        ),
        name="backward",
    )(*resident(recv, grads, exps, outs))


def exchange(x, groups=None):
    return lax.all_to_all(
        x, "seq", split_axis=0, concat_axis=0, tiled=True, axis_index_groups=groups
    )


def own_params(conv_weight, conv_bias, gain, y, core):
    rows = jnp.concatenate([conv_weight, conv_bias[None], gain[None]], axis=0)
    rows = jnp.pad(rows, ((0, ROWS - rows.shape[0]), (0, 0)))
    rows = rows.reshape(ROWS, -1, HEADS, 2, HDIM)
    rows = lax.dynamic_index_in_dim(rows, y, axis=1, keepdims=False)
    rows = lax.dynamic_index_in_dim(rows, core, axis=2, keepdims=False)
    return rows.transpose(1, 0, 2)


def sum_pair(part, x, seq):
    own = lax.dynamic_index_in_dim(part, x, axis=0, keepdims=False)
    other = lax.dynamic_index_in_dim(part, 1 - x, axis=0, keepdims=False)
    return own + lax.ppermute(other, "seq", [(i, i ^ 2) for i in range(seq)])


def sum_dp(total, dp):
    for bit in range(dp.bit_length() - 1):
        total = total + lax.ppermute(total, "dp", [(i, i ^ (1 << bit)) for i in range(dp)])
    return total


def per_device(queries, keys, values, out_grad, conv_weight, conv_bias, gain):
    width = queries.shape[2]
    seq, dp = lax.axis_size("seq"), lax.axis_size("dp")
    index = lax.axis_index("seq")
    y, x, core = index // 4, (index // 2) % 2, index % 2
    same_x = [[b * 4 + a * 2 + c for b in range(seq // 4) for c in range(2)] for a in range(2)]
    params = own_params(conv_weight, conv_bias, gain, y, core)
    recv = exchange(pack((queries, keys, values, out_grad), seq))
    exps, invs, outs, stats = forward(recv, params, len(same_x[0]))
    stats = exchange(stats, same_x)
    grads, part, exps = norm(width, stats, recv, params, outs, exps, invs)
    total = sum_pair(part, x, seq)
    packed = backward(recv, grads, exps, outs)
    packed, total = lax.optimization_barrier((packed, total))
    total = sum_dp(total, dp)
    query_grad, key_grad, value_grad = unpack(exchange(packed), width)
    return (query_grad, key_grad, value_grad, total[:TAPS], total[TAPS], total[TAPS + 1])


def solution(mesh):
    frames = P("dp", "seq", None)
    return jax.shard_map(
        per_device,
        mesh=mesh,
        in_specs=(frames, frames, frames, frames, P(), P(), P()),
        out_specs=(frames, frames, frames, P(None, "seq"), P("seq"), P("seq")),
        check_vma=False,
    )
```

time: 127 us -> 93.4 us (0.74); the launches traced: 127 us -> 91.8 us
  Pallas kernels: 29.9 us -> 16.9 us
  waiting for transfers between devices: 56.6 us -> 44.2 us
  blocking collectives: 9.57 us -> 0 us
  local copies, waits for them, and re-layouts: 4.42 us -> 1.28 us
  starting transfers between devices: 25.5 us -> 28.5 us
    ppermute x5, waiting for transfers between devices: 27.9 us -> 7.55 us  [the longest x4 7.54 us: sum_dp(): lax.ppermute(total, 'dp', [(i, i ^ 1 << bit) for i in range(dp)])]
    all_to_all x1 -> x0, blocking collectives: 9.57 us -> none  [exchange(): lax.all_to_all(x, 'seq', split_axis=0, concat_axis=0, tiled=True, axis_in...]
    pallas_call x3 -> x4, Pallas kernels: 20 us -> 11.6 us  [the longest x1 5.41 us: backward(): pl.pallas_call(backward_kernel, in_specs=held(4), out_specs=pl.BlockSpec(...]
    all_to_all x2 -> x3, waiting for transfers between devices: 28.7 us -> 36.6 us  [exchange(): lax.all_to_all(x, 'seq', split_axis=0, concat_axis=0, tiled=True, axis_in...]
    all_to_all x2 -> x3, starting transfers between devices: 10.1 us -> 14.7 us  [exchange(): lax.all_to_all(x, 'seq', split_axis=0, concat_axis=0, tiled=True, axis_in...]
    pallas_call x1, Pallas kernels: 9.89 us -> 5.36 us  [forward(): pl.pallas_call(functools.partial(forward_kernel, peers), in_specs=held(2)...]
    unnamed x13 -> x7, local copies, waits for them, and re-layouts: 3.16 us -> 0.02 us
    ppermute x5, starting transfers between devices: 15.4 us -> 13.9 us  [the longest x4 13.3 us: sum_dp(): lax.ppermute(total, 'dp', [(i, i ^ 1 << bit) for i in range(dp)])]
  transfers between devices with their start and end apart: 7 -> 8, of which waited for: 6 -> 7; matrix products, arithmetic and copies ran while one was open for 2% -> 1% of each run, Pallas kernels for 0% -> 6%
where the time goes in v2:
time: 93.4 us; the launch traced here: 91.8 us
  waiting for transfers between devices  44.2 us (47%)
  starting transfers between devices  28.5 us (31%)
  Pallas kernels  16.9 us (18%)
  local copies, waits for them, and re-layouts  1.28 us (1%)
    all_to_all x3, waiting for transfers between devices, exchange(): lax.all_to_all(x, 'seq', split_axis=0, concat_axis=0, tiled=True, axis_in...  36.6 us
    all_to_all x3, starting transfers between devices, exchange(): lax.all_to_all(x, 'seq', split_axis=0, concat_axis=0, tiled=True, axis_in...  14.7 us
    ppermute x4, starting transfers between devices, sum_dp(): lax.ppermute(total, 'dp', [(i, i ^ 1 << bit) for i in range(dp)])  13.3 us
    ppermute x4, waiting for transfers between devices, sum_dp(): lax.ppermute(total, 'dp', [(i, i ^ 1 << bit) for i in range(dp)])  7.54 us
    pallas_call x1, Pallas kernels, backward(): pl.pallas_call(backward_kernel, in_specs=held(4), out_specs=pl.BlockSpec(...  5.41 us
    pallas_call x1, Pallas kernels, forward(): pl.pallas_call(functools.partial(forward_kernel, peers), in_specs=held(2)...  5.36 us
    pallas_call x1, Pallas kernels, norm(): pl.pallas_call(functools.partial(norm_kernel, width), in_specs=held(4) +...  2.58 us
    pallas_call x1, Pallas kernels, pack(): pl.pallas_call(pack_kernel, in_specs=[pl.BlockSpec(memory_space=pltpu.HBM...  2.44 us
  transfers between devices with their start and end apart: 8, of which 7 were waited for; matrix products, arithmetic and copies ran while one was open for 1% of the time, Pallas kernels for 6%

profile of v2, /device:TPU:2, one launch (start us, length us, event | category | flops | bytes accessed | tf_op | source)
XLA Modules:
  0.0 91.8 jit_solution(17800492839664627680)
XLA Ops:
  0.6 2.4 %pack.1 = bf16[4,2,2,4,2,64,128]{6,5,4,3,2,1,0:T(8,128)(2,1)} custom-call(bf16[2,64,2048]{2,1,0:T(8,128)(2,1)} %refs_0_.1, bf16[2,64,2048]{2,1,0:T(8,128)(2,1)} %refs_1_.1, bf16[2,64,2048]{2,1,0:T(8,128)(2,1)} %refs_2_.1, bf16[2,64,2048]{2,1,0:T(8,128)(2,1)} %refs_3_.1), custom_call_target="tpu_custom_call" | custom-call | tf_op jit(solution)/shard_map/pack/pallas_call | solution.py:61
  3.1 0.0 copy-start.1
  3.1 6.3 %all-to-all-start = ((bf16[16,4,2,64,128]{4,3,2,1,0:T(8,128)(2,1)}), bf16[16,4,2,64,128]{4,3,2,1,0:T(8,128)(2,1)S(1)}, u32[]{:S(2)}, u32[]{:S(2)}) async-start(bf16[16,4,2,64,128]{4,3,2,1,0:T(8,128)(2,1)} %bitcast.20), calls=%async_computation | async-start | bytes 4194304 | tf_op jit(solution)/shard_map/all_to_all | solution.py:372
  9.5 0.1 reshape.24
  9.7 29.3 %all-to-all-done.recv = bf16[16,4,2,64,128]{4,3,2,1,0:T(8,128)(2,1)S(1)} async-done(((bf16[16,4,2,64,128]{4,3,2,1,0:T(8,128)(2,1)}), bf16[16,4,2,64,128]{4,3,2,1,0:T(8,128)(2,1)S(1)}, u32[]{:S(2)}, u32[]{:S(2)}) %all-to-all-start) | async-done | bytes 2097184 | tf_op jit(solution)/shard_map/all_to_all | solution.py:372
  39.0 5.4 %forward.1 = (bf16[2,1024,1024]{2,1,0:T(8,128)(2,1)}, f32[2,1024,128]{2,1,0:T(8,128)}, f32[2,1024,128]{2,1,0:T(8,128)S(1)}, f32[8,16,128]{2,1,0:T(8,128)}) custom-call(bf16[16,4,2,64,128]{4,3,2,1,0:T(8,128)(2,1)S(1)} %all-to-all-done.recv, f32[2,16,128]{2,1,0:T(8,128)S(1)} %bitcast.18), custom_call_target="tpu_custom_call" | custom-call | tf_op jit(solution)/shard_map/forward/pallas_call | solution.py:299
  44.4 3.4 %all-to-all-start.1 = ((f32[8,16,128]{2,1,0:T(8,128)}), f32[8,16,128]{2,1,0:T(8,128)S(1)}, u32[]{:S(2)}, u32[]{:S(2)}) async-start(f32[8,16,128]{2,1,0:T(8,128)} %get-tuple-element.18), calls=%async_computation.1 | async-start | bytes 131072 | tf_op jit(solution)/shard_map/all_to_all | solution.py:372
  47.8 5.5 %all-to-all-done.1.stats = f32[8,16,128]{2,1,0:T(8,128)S(1)} async-done(((f32[8,16,128]{2,1,0:T(8,128)}), f32[8,16,128]{2,1,0:T(8,128)S(1)}, u32[]{:S(2)}, u32[]{:S(2)}) %all-to-all-start.1) | async-done | bytes 65568 | tf_op jit(solution)/shard_map/all_to_all | solution.py:372
  53.3 2.6 %norm.1 = (bf16[2,1024,128]{2,1,0:T(8,128)(2,1)S(1)}, f32[2,16,128]{2,1,0:T(8,128)S(1)}, bf16[2,1024,1024]{2,1,0:T(8,128)(2,1)S(1)}) custom-call(f32[8,16,128]{2,1,0:T(8,128)S(1)} %all-to-all-done.1.stats, bf16[16,4,2,64,128]{4,3,2,1,0:T(8,128)(2,1)S(1)} %all-to-all-done.recv, f32[2,16,128]{2,1,0:T(8,128)S(1)} %bitcast.19, ...), custom_call_target="tpu_custom_call" | custom-call | tf_op jit(solution)/shard_map/norm/pallas_call | solution.py:325
  55.9 0.6 collective-permute-start
  56.5 5.4 %backward.1 = bf16[16,3,2,64,128]{4,3,2,1,0:T(8,128)(2,1)} custom-call(bf16[16,4,2,64,128]{4,3,2,1,0:T(8,128)(2,1)S(1)} %all-to-all-done.recv, bf16[2,1024,128]{2,1,0:T(8,128)(2,1)S(1)} %get-tuple-element.22.grads, bf16[2,1024,1024]{2,1,0:T(8,128)(2,1)S(1)} %get-tuple-element.23.exps, f32[2,1024,128]{2,1,0:T(8,128)S(1)} %get-tuple-element.19.outs), custom_call_target="tpu_custom_call" | custom-call | flops 4294967296 | bytes 16777216 | tf_op jit(solution)/shard_map/backward/pallas_call | solution.py:353
  61.9 5.0 %all-to-all-start.2 = ((bf16[16,3,2,64,128]{4,3,2,1,0:T(8,128)(2,1)}), bf16[16,3,2,64,128]{4,3,2,1,0:T(8,128)(2,1)S(1)}, u32[]{:S(2)}, u32[]{:S(2)}) async-start(bf16[16,3,2,64,128]{4,3,2,1,0:T(8,128)(2,1)} %backward.1), calls=%async_computation.2 | async-start | bytes 3145728 | tf_op jit(solution)/shard_map/all_to_all | solution.py:372
  66.9 2.0 %collective-permute-start.1 = (f32[16,128]{1,0:T(8,128)S(1)}, f32[16,128]{1,0:T(8,128)S(1)}, u32[]{:S(2)}, u32[]{:S(2)}) collective-permute-start(f32[16,128]{1,0:T(8,128)S(1)} %bitcast_add_fusion), channel_id=1, source_target_pairs={{0,16},{16,0},{32,48},{48,32},{64,80},{80,64},{96,112},{112,96},{1... | collective-permute-start | bytes 24584 | tf_op jit(solution)/shard_map/ppermute | solution.py:394
  68.9 1.7 %collective-permute-done.1 = f32[16,128]{1,0:T(8,128)S(1)} collective-permute-done((f32[16,128]{1,0:T(8,128)S(1)}, f32[16,128]{1,0:T(8,128)S(1)}, u32[]{:S(2)}, u32[]{:S(2)}) %collective-permute-start.1) | collective-permute-done | bytes 8224 | tf_op jit(solution)/shard_map/ppermute | solution.py:394
  70.7 3.3 %collective-permute-start.2 = (f32[16,128]{1,0:T(8,128)S(1)}, f32[16,128]{1,0:T(8,128)S(1)}, u32[]{:S(2)}, u32[]{:S(2)}) collective-permute-start(f32[16,128]{1,0:T(8,128)S(1)} %add.54), channel_id=1, source_target_pairs={{0,32},{16,48},{32,0},{48,16},{64,96},{80,112},{96,64},{112,80},{1... | collective-permute-start | bytes 24584 | tf_op jit(solution)/shard_map/ppermute | solution.py:394
  73.9 1.6 %collective-permute-done.2 = f32[16,128]{1,0:T(8,128)S(1)} collective-permute-done((f32[16,128]{1,0:T(8,128)S(1)}, f32[16,128]{1,0:T(8,128)S(1)}, u32[]{:S(2)}, u32[]{:S(2)}) %collective-permute-start.2) | collective-permute-done | bytes 8224 | tf_op jit(solution)/shard_map/ppermute | solution.py:394
  75.6 6.8 %collective-permute-start.3 = (f32[16,128]{1,0:T(8,128)S(1)}, f32[16,128]{1,0:T(8,128)S(1)}, u32[]{:S(2)}, u32[]{:S(2)}) collective-permute-start(f32[16,128]{1,0:T(8,128)S(1)} %add.55), channel_id=1, source_target_pairs={{0,64},{16,80},{32,96},{48,112},{64,0},{80,16},{96,32},{112,48},{1... | collective-permute-start | bytes 24584 | tf_op jit(solution)/shard_map/ppermute | solution.py:394
  82.4 1.6 %collective-permute-done.3 = f32[16,128]{1,0:T(8,128)S(1)} collective-permute-done((f32[16,128]{1,0:T(8,128)S(1)}, f32[16,128]{1,0:T(8,128)S(1)}, u32[]{:S(2)}, u32[]{:S(2)}) %collective-permute-start.3) | collective-permute-done | bytes 8224 | tf_op jit(solution)/shard_map/ppermute | solution.py:394
  84.1 1.2 %collective-permute-start.4 = (f32[16,128]{1,0:T(8,128)S(1)}, f32[16,128]{1,0:T(8,128)S(1)}, u32[]{:S(2)}, u32[]{:S(2)}) collective-permute-start(f32[16,128]{1,0:T(8,128)S(1)} %add.56), channel_id=1, source_target_pairs={{0,128},{16,144},{32,160},{48,176},{64,192},{80,208},{96,224},{112... | collective-permute-start | bytes 24584 | tf_op jit(solution)/shard_map/ppermute | solution.py:394
  85.2 2.6 %collective-permute-done.4 = f32[16,128]{1,0:T(8,128)S(1)} collective-permute-done((f32[16,128]{1,0:T(8,128)S(1)}, f32[16,128]{1,0:T(8,128)S(1)}, u32[]{:S(2)}, u32[]{:S(2)}) %collective-permute-start.4) | collective-permute-done | bytes 8224 | tf_op jit(solution)/shard_map/ppermute | solution.py:394
  87.8 0.6 slice.12
  88.4 0.5 slice_bitcast_fusion
  88.9 1.8 %all-to-all-done.2 = bf16[16,3,2,64,128]{4,3,2,1,0:T(8,128)(2,1)S(1)} async-done(((bf16[16,3,2,64,128]{4,3,2,1,0:T(8,128)(2,1)}), bf16[16,3,2,64,128]{4,3,2,1,0:T(8,128)(2,1)S(1)}, u32[]{:S(2)}, u32[]{:S(2)}) %all-to-all-start.2) | async-done | bytes 1572896 | tf_op jit(solution)/shard_map/all_to_all | solution.py:372
  90.7 1.1 %unpack.1 = (bf16[2,64,2048]{2,1,0:T(8,128)(2,1)}, bf16[2,64,2048]{2,1,0:T(8,128)(2,1)}, bf16[2,64,2048]{2,1,0:T(8,128)(2,1)}) custom-call(bf16[4,2,2,3,2,64,128]{6,5,4,3,2,1,0:T(8,128)(2,1)S(1)} %bitcast.17), custom_call_target="tpu_custom_call" | custom-call | tf_op jit(solution)/shard_map/unpack/pallas_call | solution.py:79
  (15 shorter events, 0.1 us)
Async XLA Ops:
  3.1 6.4 %copy-start = (f32[7,2048]{1,0:T(8,128)S(1)}, f32[7,2048]{1,0:T(8,128)}, u32[]{:S(2)}) copy-start(f32[7,2048]{1,0:T(8,128)} %param.11) | copy-start | bytes 172036
  3.1 6.4 %copy-start.1 = (f32[2048]{0:T(1024)S(1)}, f32[2048]{0:T(1024)}, u32[]{:S(2)}) copy-start(f32[2048]{0:T(1024)} %param.13) | copy-start | bytes 24580
  3.1 6.4 %copy-start.2 = (f32[2048]{0:T(1024)S(1)}, f32[2048]{0:T(1024)}, u32[]{:S(2)}) copy-start(f32[2048]{0:T(1024)} %param.12) | copy-start | bytes 24580
  3.1 35.9 %all-to-all-start = ((bf16[16,4,2,64,128]{4,3,2,1,0:T(8,128)(2,1)}), bf16[16,4,2,64,128]{4,3,2,1,0:T(8,128)(2,1)S(1)}, u32[]{:S(2)}, u32[]{:S(2)}) async-start(bf16[16,4,2,64,128]{4,3,2,1,0:T(8,128)(2,1)} %bitcast.20), calls=%async_computation | async-start | bytes 4194304 | tf_op jit(solution)/shard_map/all_to_all | solution.py:372
  44.4 8.9 %all-to-all-start.1 = ((f32[8,16,128]{2,1,0:T(8,128)}), f32[8,16,128]{2,1,0:T(8,128)S(1)}, u32[]{:S(2)}, u32[]{:S(2)}) async-start(f32[8,16,128]{2,1,0:T(8,128)} %get-tuple-element.18), calls=%async_computation.1 | async-start | bytes 131072 | tf_op jit(solution)/shard_map/all_to_all | solution.py:372
  55.9 6.0 %collective-permute-start = (f32[16,128]{1,0:T(8,128)S(1)}, f32[16,128]{1,0:T(8,128)S(1)}, u32[]{:S(2)}, u32[]{:S(2)}) collective-permute-start(f32[16,128]{1,0:T(8,128)S(1)} %dynamic-slice_bitcast_fusion), channel_id=1, source_target_pairs={{0,2},{1,3},{2,0},{3,1},{4,6},{5,7},{6,4},{7,5},{8,10},{9,11},{10,... | collective-permute-start | bytes 24584 | tf_op jit(solution)/shard_map/ppermute | solution.py:389
  61.9 28.8 %all-to-all-start.2 = ((bf16[16,3,2,64,128]{4,3,2,1,0:T(8,128)(2,1)}), bf16[16,3,2,64,128]{4,3,2,1,0:T(8,128)(2,1)S(1)}, u32[]{:S(2)}, u32[]{:S(2)}) async-start(bf16[16,3,2,64,128]{4,3,2,1,0:T(8,128)(2,1)} %backward.1), calls=%async_computation.2 | async-start | bytes 3145728 | tf_op jit(solution)/shard_map/all_to_all | solution.py:372
  66.9 3.7 %collective-permute-start.1 = (f32[16,128]{1,0:T(8,128)S(1)}, f32[16,128]{1,0:T(8,128)S(1)}, u32[]{:S(2)}, u32[]{:S(2)}) collective-permute-start(f32[16,128]{1,0:T(8,128)S(1)} %bitcast_add_fusion), channel_id=1, source_target_pairs={{0,16},{16,0},{32,48},{48,32},{64,80},{80,64},{96,112},{112,96},{1... | collective-permute-start | bytes 24584 | tf_op jit(solution)/shard_map/ppermute | solution.py:394
  70.7 4.9 %collective-permute-start.2 = (f32[16,128]{1,0:T(8,128)S(1)}, f32[16,128]{1,0:T(8,128)S(1)}, u32[]{:S(2)}, u32[]{:S(2)}) collective-permute-start(f32[16,128]{1,0:T(8,128)S(1)} %add.54), channel_id=1, source_target_pairs={{0,32},{16,48},{32,0},{48,16},{64,96},{80,112},{96,64},{112,80},{1... | collective-permute-start | bytes 24584 | tf_op jit(solution)/shard_map/ppermute | solution.py:394
  75.6 8.5 %collective-permute-start.3 = (f32[16,128]{1,0:T(8,128)S(1)}, f32[16,128]{1,0:T(8,128)S(1)}, u32[]{:S(2)}, u32[]{:S(2)}) collective-permute-start(f32[16,128]{1,0:T(8,128)S(1)} %add.55), channel_id=1, source_target_pairs={{0,64},{16,80},{32,96},{48,112},{64,0},{80,16},{96,32},{112,48},{1... | collective-permute-start | bytes 24584 | tf_op jit(solution)/shard_map/ppermute | solution.py:394
  84.1 3.7 %collective-permute-start.4 = (f32[16,128]{1,0:T(8,128)S(1)}, f32[16,128]{1,0:T(8,128)S(1)}, u32[]{:S(2)}, u32[]{:S(2)}) collective-permute-start(f32[16,128]{1,0:T(8,128)S(1)} %add.56), channel_id=1, source_target_pairs={{0,128},{16,144},{32,160},{48,176},{64,192},{80,208},{96,224},{112... | collective-permute-start | bytes 24584 | tf_op jit(solution)/shard_map/ppermute | solution.py:394
